TPU v7x, 512 devices: a whole 4x8x8 slice. The times are simulated.
512 devices in a mesh: dp: 32 (over y_hi, x, core), ctx: 16 (over z, y_lo).
Axes of the slice: x: 4, y: 8 (y_hi: 4, y_lo: 2; y = y_hi * 2 + y_lo), z: 8, core: 2. Of those that a mesh axis runs over, the one named last changes fastest.
Arguments:
- query: bfloat16 [32, 2048, 4096], P('dp', 'ctx'), may hold values from -6 to 6
- grad_out: bfloat16 [32, 2048, 4096], P('dp', 'ctx'), may hold values from -0.75 to 0.75
- keys: bfloat16 [32, 2048, 512], P('dp', 'ctx'), may hold values from -6 to 6
- values: bfloat16 [32, 2048, 512], P('dp', 'ctx'), may hold values from -6 to 6
- log_norm: float32 [32, 2048, 32], P('dp', 'ctx'), may hold values from 4 to 8
- row_dots: float32 [32, 2048, 32], P('dp', 'ctx'), may hold values from -6 to 6
- block_input: bfloat16 [32, 2048, 4096], P('dp', 'ctx'), may hold values from -6 to 6
- route_index: int32 [32, 2048], P('dp', 'ctx'), may hold values from 0 to 1023, as said below
- counts: int32 [32, 16], P('dp', 'ctx'), may hold values from 32 to 128, as said below
Outputs:
- key_weight_grad: float32 [4096, 512], P('ctx', 'dp')
Inputs may be any that keep to these rules, and one draw needn't show every extreme that they name: `route_index`: within each shard of 128 slots, the first counts slots hold distinct token indices in increasing order; the remaining slots hold 0 and are padding. `counts`: in every sequence one shard is full (128) and another holds 32.
All inputs are finite; a program needn't handle non-finite values.
Results may differ from a plain program's by a relative error of at most 0.004.
Values may be sent and summed in bfloat16 or wider, within the bound.
No kernel may reach another device: no remote copies, remote signals or barrier semaphores. Data moves between devices by JAX's collectives and lax.ppermute only.
A program may use at most 64 MiB of HBM per device.

v0:
```python
import jax
import jax.numpy as jnp
from jax import lax
from jax.sharding import PartitionSpec as P

HQ = 32
KVH = 4
DH = 128
TOK_DEV = 1024


far_slot = 1073741824


def head_terms(q_rows, d_rows, norms, dots, q_pos, k_rows, v_rows, k_pos):
    count = q_rows.shape[0]
    number = k_rows.shape[0]
    group = HQ // KVH
    scale = DH ** (-0.5)
    query_heads = q_rows.reshape(count, KVH, group, DH)
    grad_heads = d_rows.reshape(count, KVH, group, DH)
    key_heads = k_rows.reshape(number, KVH, DH)
    value_heads = v_rows.reshape(number, KVH, DH)
    scores = (
        jnp.einsum("rgie,tge->girt", query_heads, key_heads, preferred_element_type=jnp.float32)
        * scale
    )
    norm_cols = jnp.transpose(norms.reshape(count, KVH, group), (1, 2, 0))[..., None]
    dot_cols = jnp.transpose(dots.reshape(count, KVH, group), (1, 2, 0))[..., None]
    allowed = k_pos[None, :] <= q_pos[:, None]
    probs = jnp.where(allowed, jnp.exp(scores - norm_cols), 0.0)
    dprobs = jnp.einsum(
        "rgie,tge->girt", grad_heads, value_heads, preferred_element_type=jnp.float32
    )
    dscores = (probs * (dprobs - dot_cols)).astype(jnp.bfloat16)
    terms = jnp.einsum("girt,rgie->tge", dscores, query_heads, preferred_element_type=jnp.float32)
    return terms.reshape(number, KVH * DH)


def body(query, grad_out, keys, values, log_norm, row_dots, block_input, route_index, counts):
    capacity = query.shape[1]
    key_width = keys.shape[2]
    shards = lax.axis_size("ctx")
    seq_rows = capacity * shards
    scale = DH ** (-0.5)
    ctx_at = lax.axis_index("ctx")
    slot_ids = jnp.arange(capacity, dtype=jnp.int32)
    is_valid = slot_ids < counts[0, 0]
    position = ctx_at * TOK_DEV + route_index[0]
    key_place = jnp.where(is_valid, position, jnp.int32(far_slot))
    query_place = jnp.where(is_valid, position, jnp.int32(-1))
    all_place = lax.all_gather(key_place, "ctx", axis=0, tiled=True)
    q_rows = query[0]
    d_rows = grad_out[0]
    norms = log_norm[0]
    dots = row_dots[0]
    groups = []
    groups.append((q_rows, d_rows, norms, dots, query_place))
    latest = [jnp.max(member[4]) for member in groups]
    empty = jnp.zeros((seq_rows, key_width), jnp.float32)
    k_piece = lax.all_gather(keys[0], "ctx", axis=0, tiled=True)
    v_piece = lax.all_gather(values[0], "ctx", axis=0, tiled=True)
    count = k_piece.shape[0]
    step = 256

    def one_block(index, carried):
        begin = index * step
        k_block = lax.dynamic_slice_in_dim(k_piece, begin, step, 0)
        v_block = lax.dynamic_slice_in_dim(v_piece, begin, step, 0)
        k_pos = lax.dynamic_slice_in_dim(all_place, begin, step, 0)
        term = jnp.zeros((step, key_width), jnp.float32)
        for member, top in zip(groups, latest):
            term = lax.cond(
                jnp.min(k_pos) > top,
                lambda: jnp.zeros((step, key_width), jnp.float32),
                lambda: head_terms(
                    member[0], member[1], member[2], member[3], member[4], k_block, v_block, k_pos
                ),
            )
        former = lax.dynamic_slice_in_dim(carried, begin, step, 0)
        return lax.dynamic_update_slice_in_dim(carried, former + term, begin, 0)

    partial_grads = lax.fori_loop(0, count // step, one_block, empty)
    summed = lax.psum(partial_grads, "ctx")
    key_grad = (summed * scale).astype(jnp.bfloat16)
    columns = lax.all_to_all(block_input[0], "ctx", split_axis=1, concat_axis=0, tiled=True)
    local_grad = lax.dot_general(
        columns, key_grad, (((0,), (0,)), ((), ())), preferred_element_type=jnp.float32
    )
    result = lax.psum_scatter(local_grad, "dp", scatter_dimension=1, tiled=True)
    return result


def solution(mesh):
    in_specs = (
        P("dp", "ctx", None),
        P("dp", "ctx", None),
        P("dp", "ctx", None),
        P("dp", "ctx", None),
        P("dp", "ctx", None),
        P("dp", "ctx", None),
        P("dp", "ctx", None),
        P("dp", "ctx"),
        P("dp", "ctx"),
    )
    out_specs = P("ctx", "dp")
    return jax.shard_map(body, mesh=mesh, in_specs=in_specs, out_specs=out_specs, check_vma=False)
```

profile of v0, /device:TPU:1, one launch (start us, length us, event | category | flops | bytes accessed | tf_op | source)
XLA Modules:
  0.0 592.3 jit_solution(15844114293094117426)
XLA Ops:
  6.5 0.0 copy-start
  6.5 0.0 all-gather.6.cloned.1.call-start
  6.5 1.7 copy.33
  8.3 0.0 all-gather.6.cloned.1.call-update
  8.3 0.0 all-gather.8.cloned.1.call-start
  8.4 1.7 copy.34
  10.0 0.0 all-gather.8.cloned.1.call-update
  10.1 0.0 all-reduce.2.cloned.1.call-start
  10.8 1.6 copy.35
  12.4 1.3 fusion.15
  13.7 33.8 %all-gather.2 = s32[16,1,128]{2,1,0:T(1,128)S(1)} all-gather(s32[1,1,128]{2,1,0:T(1,128)S(1)} %get-tuple-element.352), channel_id=1, replica_groups=mesh['dp'=32,'ctx'=16] {'ctx'}, dimensions={0}, use_global_device_ids=true | all-gather | bytes 8704 | tf_op jit(solution)/shard_map/all_gather | solution.py:52
  47.4 38.8 %all-gather.6.cloned.1.call-done = bf16[1,2048,512]{1,2,0:T(8,128)(2,1)} async-done(((bf16[1,128,512]{1,2,0:T(8,128)(2,1)}), bf16[1,2048,512]{1,2,0:T(8,128)(2,1)}) %all-gather.6.cloned.1.call-update) | async-done | bytes 2097168 | tf_op jit(solution)/shard_map/all_gather | solution.py:61
  86.2 80.0 %all-gather.8.cloned.1.call-done = bf16[1,2048,512]{1,2,0:T(8,128)(2,1)} async-done(((bf16[1,128,512]{1,2,0:T(8,128)(2,1)}), bf16[1,2048,512]{1,2,0:T(8,128)(2,1)}) %all-gather.8.cloned.1.call-update) | async-done | bytes 2097168 | tf_op jit(solution)/shard_map/all_gather | solution.py:62
  166.2 2.5 broadcast_in_dim.26
  168.7 0.0 copy-done
  168.7 0.0 copy-done.2
  168.7 0.0 copy-done.3
  168.7 47.0 %while.13 = (s32[]{:T(128)}, f32[2048,512]{0,1:T(8,128)}, s32[2048]{0:T(1024)S(1)}, s32[]{:T(128)}, s32[128]{0:T(128)S(1)}, /*index=5*/bf16[2048,512]{0,1:T(8,12...) while((s32[]{:T(128)}, f32[2048,512]{0,1:T(8,128)}, ...), condition=%wide.region_5.6_spmd, body=%wide.region_1.5_spmd.sunk | while | flops 811761920 | bytes 17404196 | solution.py:83
  168.7 0.7 fusion.23
  170.5 9.2 %conditional.2 = (f32[256,512]{0,1:T(8,128)}) conditional(s32[]{:T(128)} %convert_element_type.24, (s32[256]{0:T(256)S(1)}, s32[128]{0:T(128)S(1)}, bf16[2048,512]{0,1:T(8,128)(2,1)}, s32[]{:T(128)}, bf16[1,128,4096]{1,2,0:T(8,128)(2,1)S(1)}, /*index=5*/f32[1,128,32]{1,2,0:T(8,128)S(1)}, bf16[2048,512]{0,1:T(8,128)(2,1)}, ...), branch_computations={%region_3.3_spmd, %region_4.4_spmd} | conditional | flops 811630592 | bytes 15828492 | solution.py:73
  170.6 1.1 constant_dynamic-slice_fusion
  171.6 2.7 fusion.16
  174.3 0.2 copy.47
  174.6 0.1 broadcast_compare_fusion
  174.7 5.0 fusion.4
  179.7 2.2 add_dynamic-update-slice_fusion.2
  181.9 0.7 fusion.23
  183.7 0.9 conditional.2
  183.7 0.8 broadcast.15
  184.6 2.1 add_dynamic-update-slice_fusion.2
  186.7 0.7 fusion.23
  188.6 0.9 conditional.2
  188.6 0.8 broadcast.15
  189.4 2.2 add_dynamic-update-slice_fusion.2
  191.6 0.7 fusion.23
  193.4 0.9 conditional.2
  193.5 0.8 broadcast.15
  194.3 2.1 add_dynamic-update-slice_fusion.2
  196.4 0.7 fusion.23
  198.3 0.9 conditional.2
  198.3 0.8 broadcast.15
  199.1 2.1 add_dynamic-update-slice_fusion.2
  201.3 0.7 fusion.23
  203.1 0.9 conditional.2
  203.1 0.8 broadcast.15
  204.0 2.1 add_dynamic-update-slice_fusion.2
  206.1 0.7 fusion.23
  207.9 0.9 conditional.2
  207.9 0.8 broadcast.15
  208.8 2.1 add_dynamic-update-slice_fusion.2
  210.9 0.7 fusion.23
  212.7 0.9 conditional.2
  212.8 0.8 broadcast.15
  213.6 2.1 add_dynamic-update-slice_fusion.2
  215.7 0.0 all-reduce.2.cloned.1.call-update
  215.7 0.0 reduce-scatter.2.cloned.1.call-start
  215.8 1.1 copy-done.1
  216.9 0.7 copy.36
  217.6 80.3 %all_to_all.19 = bf16[128,16,256]{0,2,1:T(8,128)(2,1)S(1)} all-to-all(bf16[128,16,256]{0,2,1:T(8,128)(2,1)S(1)} %bitcast.74), channel_id=1, replica_groups=mesh['dp'=32,'ctx'=16] {'ctx'}, dimensions={1} | all-to-all | bytes 2097152 | tf_op jit(solution)/shard_map/all_to_all | solution.py:86
  297.8 0.5 copy.37
  298.4 190.9 %all-reduce.2.cloned.1.call-done = f32[2048,512]{0,1:T(8,128)} async-done(((f32[2048,512]{0,1:T(8,128)}), f32[2048,512]{0,1:T(8,128)}) %all-reduce.2.cloned.1.call-update) | async-done | bytes 4194320 | tf_op jit(solution)/shard_map/psum | solution.py:84
  489.2 3.7 fusion.11
  492.9 0.0 reduce-scatter.2.cloned.1.call-update
  493.0 92.8 %reduce-scatter.2.cloned.1.call-done = f32[256,16]{0,1:T(8,128)} async-done(((f32[256,512]{0,1:T(8,128)}), f32[256,16]{0,1:T(8,128)}) %reduce-scatter.2.cloned.1.call-update) | async-done | bytes 16400 | tf_op jit(solution)/shard_map/reduce_scatter | solution.py:90
  (3 shorter events, 0.0 us)
Async XLA Ops:
  6.5 162.1 %copy-start = (bf16[1,128,4096]{2,1,0:T(8,128)(2,1)S(1)}, bf16[1,128,4096]{2,1,0:T(8,128)(2,1)}, u32[]{:S(2)}) copy-start(bf16[1,128,4096]{2,1,0:T(8,128)(2,1)} %param.14) | copy-start | bytes 3145732
  6.5 162.1 %copy-start.2 = (f32[1,128,32]{1,2,0:T(8,128)S(1)}, f32[1,128,32]{1,2,0:T(8,128)}, u32[]{:S(2)}) copy-start(f32[1,128,32]{1,2,0:T(8,128)} %param.17) | copy-start | bytes 49156
  6.5 162.1 %copy-start.3 = (f32[1,128,32]{1,2,0:T(8,128)S(1)}, f32[1,128,32]{1,2,0:T(8,128)}, u32[]{:S(2)}) copy-start(f32[1,128,32]{1,2,0:T(8,128)} %param.18) | copy-start | bytes 49156
  6.5 79.7 %all-gather.6.cloned.1.call-start = ((), (), s32[]{:S(2)}) async-start(), calls=%async_computation.4 | async-start | bytes 2228224 | tf_op jit(solution)/shard_map/all_gather | solution.py:61
  8.3 157.9 %all-gather.8.cloned.1.call-start = ((), (), s32[]{:S(2)}) async-start(), calls=%async_computation.5 | async-start | bytes 2228224 | tf_op jit(solution)/shard_map/all_gather | solution.py:62
  10.1 479.2 %all-reduce.2.cloned.1.call-start = ((), (), s32[]{:S(2)}) async-start(), calls=%async_computation.2 | async-start | bytes 8388608 | tf_op jit(solution)/shard_map/psum | solution.py:84
  215.7 1.2 copy-start.1
  215.7 370.0 %reduce-scatter.2.cloned.1.call-start = ((), (), s32[]{:S(2)}) async-start(), calls=%async_computation.3 | async-start | bytes 540672 | tf_op jit(solution)/shard_map/reduce_scatter | solution.py:90
Sparse Core Ops, SparseCore 0:
  9.4 76.7 all-gather.5
  88.2 77.9 all-gather.7
  215.8 273.3 all-reduce.1
  493.4 92.2 reduce-scatter.1
where the time goes:
time: 594 us; the launch traced here: 592 us
  waiting for transfers between devices  402 us (68%)
  blocking collectives  114 us (19%)
  other arithmetic  23.8 us (4%)
  local copies, waits for them, and re-layouts  17.1 us (3%)
  between operations  13.8 us (2%)
  matrix products  11.4 us (2%)
  loops' own time  9.56 us (2%)
    psum x1, waiting for transfers between devices, body(): summed = lax.psum(partial_grads, 'ctx')  191 us
    reduce_scatter x1, waiting for transfers between devices, body(): result = lax.psum_scatter(local_grad, 'dp', scatter_dimension=1, tiled=True)  92.8 us
    all_to_all x1, blocking collectives, body(): lax.all_to_all(block_input[0], 'ctx', split_axis=1, concat_axis=0, tiled=...  80.3 us
    all_gather x1, waiting for transfers between devices, body(): v_piece = lax.all_gather(values[0], 'ctx', axis=0, tiled=True)  80 us
    all_gather x1, waiting for transfers between devices, body(): k_piece = lax.all_gather(keys[0], 'ctx', axis=0, tiled=True)  38.8 us
    all_gather x1, blocking collectives, body(): all_place = lax.all_gather(key_place, 'ctx', axis=0, tiled=True)  33.8 us
    dynamic_update_slice x8, other arithmetic, one_block(): return lax.dynamic_update_slice_in_dim(carried, former + term, begin, 0)  17 us
  transfers between devices with their start and end apart: 4, of which 4 were waited for; matrix products, arithmetic and copies ran while one was open for 1% of the time, Pallas kernels for 0%

commit v1 on v0

v1 whole, which is shorter than its diff:
```python
import functools

import jax
import jax.numpy as jnp
import numpy as np
from jax import lax
from jax.experimental import pallas as pl
from jax.experimental.pallas import tpu as pltpu
from jax.sharding import Mesh, PartitionSpec as P

HQ = 32
KVH = 4
DH = 128
GROUP = HQ // KVH
CAP = 128
D = 4096
LOG2E = 1.4426950408889634
SCALE = DH ** (-0.5)
HOME = ("zl", "yl")
HALF = GROUP // 2
CHUNK_ROWS = 2 * HALF * CAP + 32
SUPER = 4 * CAP
VMEM = 50 * 1024 * 1024


def split3(x):
    hi = x.astype(jnp.bfloat16)
    rest = x - hi.astype(jnp.float32)
    mid = rest.astype(jnp.bfloat16)
    lo = (rest - mid.astype(jnp.float32)).astype(jnp.bfloat16)
    return hi, mid, lo


def whole(*shape):
    return pl.BlockSpec(memory_space=pltpu.VMEM)


def pack_kv_kernel(count_ref, k_ref, v_ref, out_ref):
    rows = lax.broadcasted_iota(jnp.int32, (CAP, DH), 0)
    valid = rows < count_ref[0, 0]
    for g in range(KVH):
        cols = slice(g * DH, (g + 1) * DH)
        out_ref[g, 0] = jnp.where(valid, k_ref[:, cols], jnp.zeros((), jnp.bfloat16))
        out_ref[g, 1] = v_ref[:, cols]


def pack_kv(counts, keys, values):
    return pl.pallas_call(
        pack_kv_kernel,
        out_shape=jax.ShapeDtypeStruct((KVH, 2, CAP, DH), jnp.bfloat16),
        in_specs=[pl.BlockSpec(memory_space=pltpu.SMEM), whole(), whole()],
        out_specs=whole(),
        compiler_params=pltpu.CompilerParams(vmem_limit_bytes=VMEM),
        name="pack_kv",
    )(counts, keys, values)


def pack_q_kernel(chunk, count_ref, q_ref, d_ref, n_ref, t_ref, out_ref):
    g = pl.program_id(0)
    for h in range(HALF):
        cols = slice(h * DH, (h + 1) * DH)
        out_ref[0, h * CAP:(h + 1) * CAP] = q_ref[:, cols]
        out_ref[0, (HALF + h) * CAP:(HALF + h + 1) * CAP] = d_ref[:, cols]
    lane = lax.broadcasted_iota(jnp.int32, (HQ, CAP), 1)
    norms = jnp.where(lane < count_ref[0, 0], n_ref[...] * LOG2E, jnp.float32(1e30))
    dots = t_ref[...]
    base = 2 * HALF * CAP
    for which in range(KVH):

        @pl.when(g == which)
        def _():
            heads = slice(which * GROUP + chunk * HALF, which * GROUP + (chunk + 1) * HALF)
            parts = [*split3(norms[heads]), *split3(dots[heads])]
            parts.append(jnp.zeros((8, CAP), jnp.bfloat16))
            out_ref[0, base:base + 32] = jnp.concatenate(
                [p.astype(jnp.float32) for p in parts], axis=0
            ).astype(jnp.bfloat16)


def pack_q(chunk, counts, query, grad, norms_t, dots_t):
    part = lambda g: (0, 2 * g + chunk)
    return pl.pallas_call(
        functools.partial(pack_q_kernel, chunk),
        grid=(KVH,),
        out_shape=jax.ShapeDtypeStruct((KVH, CHUNK_ROWS, DH), jnp.bfloat16),
        in_specs=[
            pl.BlockSpec(memory_space=pltpu.SMEM),
            pl.BlockSpec((CAP, HALF * DH), part),
            pl.BlockSpec((CAP, HALF * DH), part),
            pl.BlockSpec((HQ, CAP), lambda g: (0, 0)),
            pl.BlockSpec((HQ, CAP), lambda g: (0, 0)),
        ],
        out_specs=pl.BlockSpec((1, CHUNK_ROWS, DH), lambda g: (g, 0, 0)),
        compiler_params=pltpu.CompilerParams(vmem_limit_bytes=VMEM),
        name="pack_q%d" % chunk,
    )(counts, query, grad, norms_t, dots_t)


def pack_x_kernel(count_ref, x_ref, out_ref):
    rows = lax.broadcasted_iota(jnp.int32, (CAP, 256), 0)
    valid = rows < count_ref[0, 0]
    for z in range(4):
        for j in range(4):
            begin = z * 1024 + j * 256
            out_ref[j, :, z * 256:(z + 1) * 256] = jnp.where(
                valid, x_ref[:, begin:begin + 256], jnp.zeros((), jnp.bfloat16)
            )


def pack_x(counts, x):
    return pl.pallas_call(
        pack_x_kernel,
        out_shape=jax.ShapeDtypeStruct((4, CAP, 1024), jnp.bfloat16),
        in_specs=[pl.BlockSpec(memory_space=pltpu.SMEM), whole()],
        out_specs=whole(),
        compiler_params=pltpu.CompilerParams(vmem_limit_bytes=VMEM),
        name="pack_x",
    )(counts, x)


NT = (((1,), (1,)), ((), ()))
NN = (((1,), (0,)), ((), ()))


def rows_of(qd_ref, j):
    base = 2 * HALF * CAP
    small = qd_ref[j, base:base + 32].astype(jnp.float32)
    norm = small[0:4] + small[4:8] + small[8:12]
    dot = small[12:16] + small[16:20] + small[20:24]
    return norm, dot


def dscores(scores, dprobs, norm, dot, keep=None):
    out = []
    for h in range(HALF):
        cols = slice(h * CAP, (h + 1) * CAP)
        p = jnp.exp2(scores[:, cols] * (SCALE * LOG2E) - norm[h:h + 1])
        if keep is not None:
            p = jnp.where(keep, p, 0.0)
        out.append((p * (dprobs[:, cols] - dot[h:h + 1])).astype(jnp.bfloat16))
    return jnp.concatenate(out, axis=1)


def attend(qd_ref, j, k, v, rows=None, keep=None):
    q = qd_ref[j, 0:HALF * CAP]
    d = qd_ref[j, HALF * CAP:2 * HALF * CAP]
    norm, dot = rows
    scores = lax.dot_general(k, q, NT, preferred_element_type=jnp.float32)
    dprobs = lax.dot_general(v, d, NT, preferred_element_type=jnp.float32)
    ds = dscores(scores, dprobs, norm, dot, keep)
    return lax.dot_general(ds, q, NN, preferred_element_type=jnp.float32)


def attend_kernel(first, place_ref, qd_ref, own_ref, r1_ref, l1_ref, ra_ref, lb_ref, *rest):
    if first:
        (out_ref,) = rest
    else:
        before_ref, out_ref = rest
    zh = place_ref[0]

    def far(dist, kv):
        at = lax.rem(zh - dist + 4, 4)

        @pl.when(zh >= dist)
        def _():
            def step(j, _):
                k, v = kv()
                term = attend(qd_ref, j, k, v, rows_of(qd_ref, j))

                @pl.when(j == 0)
                def _():
                    acc_ref = out_ref if first else before_ref
                    if first:
                        out_ref[at] = term
                    else:
                        out_ref[at] = (acc_ref[at] + term).astype(out_ref.dtype)

                @pl.when(j > 0)
                def _():
                    out_ref[at] = (out_ref[at] + term).astype(out_ref.dtype)

                return 0

            lax.fori_loop(0, 4, step, 0)

        @pl.when(zh < dist)
        def _():
            out_ref[at] = jnp.zeros((SUPER, DH), out_ref.dtype)

    def stack(ref, which):
        return ref[:, which].reshape(-1, DH)

    row = lax.broadcasted_iota(jnp.int32, (CAP, CAP), 0)
    lane = lax.broadcasted_iota(jnp.int32, (CAP, CAP), 1)
    out_ref[zh] = jnp.zeros((SUPER, DH), out_ref.dtype) if first else before_ref[zh]
    for j in range(4):
        small = rows_of(qd_ref, j)
        term = attend(qd_ref, j, own_ref[j, 0], own_ref[j, 1], small, row <= lane)
        out_ref[zh, j * CAP:(j + 1) * CAP] += term
        if j > 0:
            k = own_ref[0:j, 0].reshape(j * CAP, DH)
            v = own_ref[0:j, 1].reshape(j * CAP, DH)
            out_ref[zh, 0:j * CAP] += attend(qd_ref, j, k, v, small)
    far(1, lambda: (stack(r1_ref, 0), stack(r1_ref, 1)))
    far(3, lambda: (stack(l1_ref, 0), stack(l1_ref, 1)))
    far(
        2,
        lambda: tuple(
            jnp.concatenate([stack(ra_ref, i), stack(lb_ref, i)], axis=0) for i in range(2)
        ),
    )


def attend_call(place, qd, blocks, before=None):
    first = before is None
    args = [place, qd, *blocks] + ([] if first else [before])
    return pl.pallas_call(
        functools.partial(attend_kernel, first),
        out_shape=jax.ShapeDtypeStruct((4, SUPER, DH), jnp.float32),
        in_specs=[pl.BlockSpec(memory_space=pltpu.SMEM)] + [whole()] * (len(args) - 1),
        out_specs=whole(),
        compiler_params=pltpu.CompilerParams(vmem_limit_bytes=VMEM),
        name="attend_first" if first else "attend_next",
    )(*args)


def key_grad_kernel(part_ref, out_ref):
    total = part_ref[0].astype(jnp.float32)
    for z in range(1, 4):
        total = total + part_ref[z].astype(jnp.float32)
    grad = (total * SCALE).T.astype(jnp.bfloat16)
    for core in range(2):
        piece = jnp.concatenate(
            [grad[x * 32 + core * 16:x * 32 + core * 16 + 16] for x in range(4)], axis=0
        )
        for j in range(4):
            out_ref[core, j] = piece


def key_grad_call(parts):
    return pl.pallas_call(
        key_grad_kernel,
        out_shape=jax.ShapeDtypeStruct((2, 4, 64, SUPER), jnp.bfloat16),
        in_specs=[whole()],
        out_specs=whole(),
        compiler_params=pltpu.CompilerParams(vmem_limit_bytes=VMEM),
        name="key_grad",
    )(parts)


def project_kernel(core_ref, grad_ref, mine_ref, other_ref, out_ref):
    core = core_ref[0]
    mine = grad_ref[core].reshape(256, SUPER)
    other = grad_ref[1 - core].reshape(256, SUPER)
    total = lax.dot_general(
        mine, mine_ref[...].reshape(SUPER, 1024), NN, preferred_element_type=jnp.float32
    ) + lax.dot_general(
        other, other_ref[...].reshape(SUPER, 1024), NN, preferred_element_type=jnp.float32
    )
    total = total.astype(jnp.bfloat16)
    for c in range(16):
        for z in range(4):
            out_ref[c, z] = total[c * 16:(c + 1) * 16, z * 256:(z + 1) * 256]


def project(core, grads, mine, other):
    return pl.pallas_call(
        project_kernel,
        out_shape=jax.ShapeDtypeStruct((16, 4, 16, 256), jnp.bfloat16),
        in_specs=[pl.BlockSpec(memory_space=pltpu.SMEM)] + [whole()] * 3,
        out_specs=whole(),
        compiler_params=pltpu.CompilerParams(vmem_limit_bytes=VMEM),
        name="project",
    )(core, grads, mine, other)


def total_kernel(part_ref, out_ref):
    def step(i, total):
        return total + part_ref[i].astype(jnp.float32)

    total = part_ref[0].astype(jnp.float32)
    for i in range(1, 64):
        total = step(i, total)
    out_ref[...] = total.T


def total_call(parts):
    return pl.pallas_call(
        total_kernel,
        out_shape=jax.ShapeDtypeStruct((256, 16), jnp.float32),
        in_specs=[whole()],
        out_specs=whole(),
        compiler_params=pltpu.CompilerParams(vmem_limit_bytes=VMEM),
        name="total",
    )(parts)


def shift(x, step):
    return lax.ppermute(x, "zh", [(i, (i + step) % 4) for i in range(4)])


def body(query, grad_out, keys, values, log_norm, row_dots, block_input, route_index, counts):
    del route_index
    place = lax.axis_index("zh").reshape(1).astype(jnp.int32)
    core = lax.axis_index("core").reshape(1).astype(jnp.int32)
    kv = pack_kv(counts, keys[0], values[0])
    own = lax.all_to_all(kv, HOME, 0, 0)
    norms_t, dots_t = log_norm[0].T, row_dots[0].T
    queries = [
        lax.all_to_all(pack_q(c, counts, query[0], grad_out[0], norms_t, dots_t), HOME, 0, 0)
        for c in range(2)
    ]
    r1, l1 = shift(own, 1), shift(own, -1)
    ra, lb = shift(r1[:2], 1), shift(l1[2:], -1)
    mine = lax.all_to_all(pack_x(counts, block_input[0]), HOME, 0, 0)
    other = lax.ppermute(mine, "core", [(0, 1), (1, 0)])
    blocks = (own, r1, l1, ra, lb)
    terms = attend_call(place, queries[0], blocks)
    terms = attend_call(place, queries[1], blocks, terms)
    parts = lax.all_to_all(terms.astype(jnp.bfloat16), "zh", 0, 0)
    grads = key_grad_call(parts)
    grads = lax.all_to_all(grads.reshape(8, 64, SUPER), ("core",) + HOME, 0, 0)
    local = project(core, grads.reshape(2, 4, 64, SUPER), mine, other)
    pieces = lax.all_to_all(local.reshape(64, 16, 256), ("yh", "x", "zh"), 0, 0)
    return total_call(pieces)


def solution(mesh):
    fine = Mesh(
        np.asarray(mesh.devices).reshape(4, 4, 2, 4, 2, 2), ("yh", "x", "core", "zh", "zl", "yl")
    )
    dp, ctx = ("yh", "x", "core"), ("zh", "zl", "yl")
    in_specs = (P(dp, ctx, None),) * 7 + (P(dp, ctx),) * 2
    return jax.shard_map(body, mesh=fine, in_specs=in_specs, out_specs=P(ctx, dp), check_vma=False)
```

time: 594 us -> 185 us (0.31)
  waiting for transfers between devices: 402 us -> 50.7 us
  blocking collectives: 114 us -> 31.7 us
  starting transfers between devices: 0.13 us -> 82.3 us
  other arithmetic: 23.8 us -> 0.87 us
  between operations: 13.8 us -> 0.89 us
  Pallas kernels: 0 us -> 12.3 us
  local copies, waits for them, and re-layouts: 17.1 us -> 5.17 us
  matrix products: 11.4 us -> 0 us
  loops' own time: 9.56 us -> 0 us
    psum x1 -> x0, waiting for transfers between devices: 191 us -> none  [body(): summed = lax.psum(partial_grads, 'ctx')]
    all_gather x2 -> x0, waiting for transfers between devices: 119 us -> none  [the longest x1 80 us: body(): v_piece = lax.all_gather(values[0], 'ctx', axis=0, tiled=True)]
    reduce_scatter x1 -> x0, waiting for transfers between devices: 92.8 us -> none  [body(): result = lax.psum_scatter(local_grad, 'dp', scatter_dimension=1, tiled=True)]
    all_to_all x1, blocking collectives: 80.3 us -> 31.7 us  [body(): pieces = lax.all_to_all(local.reshape(64, 16, 256), ('yh', 'x', 'zh'), 0, 0)]
    all_to_all x0 -> x6, starting transfers between devices: none -> 48 us  [the longest x1 22.4 us: body(): parts = lax.all_to_all(terms.astype(jnp.bfloat16), 'zh', 0, 0)]
    ppermute x0 -> x5, starting transfers between devices: none -> 34.3 us  [the longest x4 29 us: shift(): return lax.ppermute(x, 'zh', [(i, (i + step) % 4) for i in range(4)])]
    all_gather x1 -> x0, blocking collectives: 33.8 us -> none  [body(): all_place = lax.all_gather(key_place, 'ctx', axis=0, tiled=True)]
    all_to_all x0 -> x6, waiting for transfers between devices: none -> 27.2 us  [the longest x2 14.1 us: body(): lax.all_to_all(pack_q(c, counts, query[0], grad_out[0], norms_t, dots_t),...]
  transfers between devices with their start and end apart: 4 -> 11, of which waited for: 4 -> 7; matrix products, arithmetic and copies ran while one was open for 1% -> 0% of each run, Pallas kernels for 0% -> 6%
where the time goes in v1:
time: 185 us; the launch traced here: 184 us
  starting transfers between devices  82.3 us (44%)
  waiting for transfers between devices  50.7 us (27%)
  blocking collectives  31.7 us (17%)
  Pallas kernels  12.3 us (7%)
  local copies, waits for them, and re-layouts  5.17 us (3%)
    all_to_all x1, blocking collectives, body(): pieces = lax.all_to_all(local.reshape(64, 16, 256), ('yh', 'x', 'zh'), 0, 0)  31.7 us
    ppermute x4, starting transfers between devices, shift(): return lax.ppermute(x, 'zh', [(i, (i + step) % 4) for i in range(4)])  29 us
    ppermute x4, waiting for transfers between devices, shift(): return lax.ppermute(x, 'zh', [(i, (i + step) % 4) for i in range(4)])  23.5 us
    all_to_all x1, starting transfers between devices, body(): parts = lax.all_to_all(terms.astype(jnp.bfloat16), 'zh', 0, 0)  22.4 us
    all_to_all x2, waiting for transfers between devices, body(): lax.all_to_all(pack_q(c, counts, query[0], grad_out[0], norms_t, dots_t),...  14.1 us
    all_to_all x1, waiting for transfers between devices, body(): grads = lax.all_to_all(grads.reshape(8, 64, SUPER), ('core',) + HOME, 0, 0)  9.05 us
    all_to_all x1, starting transfers between devices, body(): grads = lax.all_to_all(grads.reshape(8, 64, SUPER), ('core',) + HOME, 0, 0)  8.85 us
    all_to_all x2, starting transfers between devices, body(): lax.all_to_all(pack_q(c, counts, query[0], grad_out[0], norms_t, dots_t),...  8.03 us
  transfers between devices with their start and end apart: 11, of which 7 were waited for; matrix products, arithmetic and copies ran while one was open for 0% of the time, Pallas kernels for 6%

profile of v1, /device:TPU:1, one launch (start us, length us, event | category | flops | bytes accessed | tf_op | source)
XLA Modules:
  0.0 183.9 jit_solution(162906463061172846)
XLA Ops:
  0.0 0.0 copy-start
  0.7 0.0 copy-start.4
  0.8 0.9 copy-done.4
  1.6 0.0 copy-start.5
  1.7 0.9 copy-done.5
  2.6 0.8 pack_kv.1
  3.3 5.2 %all-to-all-start.1 = ((bf16[4,2,128,128]{3,2,1,0:T(8,128)(2,1)}), bf16[4,2,128,128]{3,2,1,0:T(8,128)(2,1)S(1)}, u32[]{:S(2)}, u32[]{:S(2)}) async-start(bf16[4,2,128,128]{3,2,1,0:T(8,128)(2,1)} %pack_kv.1), calls=%async_computation.1 | async-start | bytes 524288 | tf_op jit(solution)/shard_map/all_to_all | solution.py:307
  8.5 0.0 copy-done
  8.5 0.0 copy-start.1
  8.5 1.2 copy-done.1
  9.7 0.0 copy-start.6
  9.7 0.7 copy-done.6
  10.5 0.0 copy-start.8
  10.5 0.7 copy-done.8
  11.2 1.7 pack_q0.1
  12.9 0.0 copy-start.2
  12.9 0.0 copy-start.7
  12.9 0.0 copy-start.9
  12.9 0.0 all-to-all-done.1.own_ref
  12.9 3.8 %all-to-all-start.2 = ((bf16[4,1056,128]{2,1,0:T(8,128)(2,1)}), bf16[4,1056,128]{2,1,0:T(8,128)(2,1)S(1)}, u32[]{:S(2)}, u32[]{:S(2)}) async-start(bf16[4,1056,128]{2,1,0:T(8,128)(2,1)} %pack_q0.1), calls=%async_computation.2 | async-start | bytes 2162688 | tf_op jit(solution)/shard_map/all_to_all | solution.py:310
  16.7 0.0 copy-done.2
  16.7 0.0 copy-done.7
  16.7 0.0 copy-done.9
  16.7 1.8 pack_q1.1
  18.5 0.0 copy-start.3
  18.5 6.7 %all-to-all-done.2.qd_ref = bf16[4,1056,128]{2,1,0:T(8,128)(2,1)S(1)} async-done(((bf16[4,1056,128]{2,1,0:T(8,128)(2,1)}), bf16[4,1056,128]{2,1,0:T(8,128)(2,1)S(1)}, u32[]{:S(2)}, u32[]{:S(2)}) %all-to-all-start.2) | async-done | bytes 1081376 | tf_op jit(solution)/shard_map/all_to_all | solution.py:310
  25.2 4.2 %all-to-all-start = ((bf16[4,1056,128]{2,1,0:T(8,128)(2,1)}), bf16[4,1056,128]{2,1,0:T(8,128)(2,1)}, u32[]{:S(2)}, u32[]{:S(2)}) async-start(bf16[4,1056,128]{2,1,0:T(8,128)(2,1)} %pack_q1.1), calls=%async_computation | async-start | bytes 2162688 | tf_op jit(solution)/shard_map/all_to_all | solution.py:310
  29.4 0.0 copy-done.3
  29.4 1.1 pack_x.1
  30.5 7.4 %all-to-all-done.qd_ref = bf16[4,1056,128]{2,1,0:T(8,128)(2,1)} async-done(((bf16[4,1056,128]{2,1,0:T(8,128)(2,1)}), bf16[4,1056,128]{2,1,0:T(8,128)(2,1)}, u32[]{:S(2)}, u32[]{:S(2)}) %all-to-all-start) | async-done | bytes 1081376 | tf_op jit(solution)/shard_map/all_to_all | solution.py:310
  37.9 3.5 %all-to-all-start.5 = ((bf16[4,128,1024]{2,1,0:T(8,128)(2,1)}), bf16[4,128,1024]{2,1,0:T(8,128)(2,1)S(1)}, u32[]{:S(2)}, u32[]{:S(2)}) async-start(bf16[4,128,1024]{2,1,0:T(8,128)(2,1)} %pack_x.1), calls=%async_computation.5 | async-start | bytes 2097152 | tf_op jit(solution)/shard_map/all_to_all | solution.py:315
  41.5 15.7 %collective-permute-start = (bf16[4,2,128,128]{3,2,1,0:T(8,128)(2,1)S(1)}, bf16[4,2,128,128]{3,2,1,0:T(8,128)(2,1)S(1)}, u32[]{:S(2)}, u32[]{:S(2)}) collective-permute-start(bf16[4,2,128,128]{3,2,1,0:T(8,128)(2,1)S(1)} %all-to-all-done.1.own_ref), channel_id=1, source_target_pairs={{0,4},{4,8},{8,12},{12,0},{1,5},{5,9},{9,13},{13,1},{2,6},{6,10},{... | collective-permute-start | bytes 786440 | tf_op jit(solution)/shard_map/ppermute | solution.py:299
  57.2 5.9 %collective-permute-start.1 = (bf16[4,2,128,128]{3,2,1,0:T(8,128)(2,1)S(1)}, bf16[4,2,128,128]{3,2,1,0:T(8,128)(2,1)S(1)}, u32[]{:S(2)}, u32[]{:S(2)}) collective-permute-start(bf16[4,2,128,128]{3,2,1,0:T(8,128)(2,1)S(1)} %all-to-all-done.1.own_ref), channel_id=1, source_target_pairs={{0,12},{4,0},{8,4},{12,8},{1,13},{5,1},{9,5},{13,9},{2,14},{6,2},{... | collective-permute-start | bytes 786440 | tf_op jit(solution)/shard_map/ppermute | solution.py:299
  63.1 21.6 %collective-permute-done.r1_ref = bf16[4,2,128,128]{3,2,1,0:T(8,128)(2,1)S(1)} collective-permute-done((bf16[4,2,128,128]{3,2,1,0:T(8,128)(2,1)S(1)}, bf16[4,2,128,128]{3,2,1,0:T(8,128)(2,1)S(1)}, u32[]{:S(2)}, u32[]{:S(2)}) %collective-permute-start) | collective-permute-done | bytes 262176 | tf_op jit(solution)/shard_map/ppermute | solution.py:299
  84.7 1.9 %collective-permute-start.2 = (bf16[2,2,128,128]{3,2,1,0:T(8,128)(2,1)S(1)}, bf16[2,2,128,128]{3,2,1,0:T(8,128)(2,1)S(1)}, u32[]{:S(2)}, u32[]{:S(2)}) collective-permute-start(bf16[2,2,128,128]{3,2,1,0:T(8,128)(2,1)S(1)} %slice.8), channel_id=1, source_target_pairs={{0,4},{4,8},{8,12},{12,0},{1,5},{5,9},{9,13},{13,1},{2,6},{6,10},{... | collective-permute-start | bytes 393224 | tf_op jit(solution)/shard_map/ppermute | solution.py:299
  86.6 0.0 collective-permute-done.1.l1_ref
  86.6 5.5 %collective-permute-start.3 = (bf16[2,2,128,128]{3,2,1,0:T(8,128)(2,1)S(1)}, bf16[2,2,128,128]{3,2,1,0:T(8,128)(2,1)S(1)}, u32[]{:S(2)}, u32[]{:S(2)}) collective-permute-start(bf16[2,2,128,128]{3,2,1,0:T(8,128)(2,1)S(1)} %slice.9), channel_id=1, source_target_pairs={{0,12},{4,0},{8,4},{12,8},{1,13},{5,1},{9,5},{13,9},{2,14},{6,2},{... | collective-permute-start | bytes 393224 | tf_op jit(solution)/shard_map/ppermute | solution.py:299
  92.1 0.4 collective-permute-done.2.ra_ref
  92.5 1.5 collective-permute-done.3.lb_ref
  94.0 1.9 %attend_first.1.rest_0_ = f32[4,512,128]{2,1,0:T(8,128)S(1)} custom-call(s32[1]{0:T(128)} %bitcast.1.place_ref, bf16[4,1056,128]{2,1,0:T(8,128)(2,1)S(1)} %all-to-all-done.2.qd_ref, bf16[4,2,128,128]{3,2,1,0:T(8,128)(2,1)S(1)} %all-to-all-done.1.own_ref, bf16[4,2,128,128]{3,2,1,0:T(8,128)(2,1)S(1)} %collective-permute-done.r1_ref, ...), custom_call_target="tpu_custom_call" | custom-call | tf_op jit(solution)/shard_map/attend_first/pallas_call | solution.py:217
  96.0 3.2 %attend_next.1 = f32[4,512,128]{2,1,0:T(8,128)S(1)} custom-call(s32[1]{0:T(128)} %bitcast.1.place_ref, bf16[4,1056,128]{2,1,0:T(8,128)(2,1)} %all-to-all-done.qd_ref, bf16[4,2,128,128]{3,2,1,0:T(8,128)(2,1)S(1)} %all-to-all-done.1.own_ref, bf16[4,2,128,128]{3,2,1,0:T(8,128)(2,1)S(1)} %collective-permute-done.r1_ref, ...), custom_call_target="tpu_custom_call" | custom-call | tf_op jit(solution)/shard_map/attend_next/pallas_call | solution.py:217
  99.1 0.9 convert_element_type.3
  100.0 0.0 all-to-all-done.5.mine_ref
  100.0 22.4 %all-to-all-start.3 = ((bf16[4,512,128]{2,1,0:T(8,128)(2,1)}), bf16[4,512,128]{2,1,0:T(8,128)(2,1)S(1)}, u32[]{:S(2)}, u32[]{:S(2)}) async-start(bf16[4,512,128]{2,1,0:T(8,128)(2,1)} %convert_element_type.3), calls=%async_computation.3 | async-start | bytes 1048576 | tf_op jit(solution)/shard_map/all_to_all | solution.py:320
  122.4 5.3 %collective-permute-start.4 = (bf16[4,128,1024]{2,1,0:T(8,128)(2,1)S(1)}, bf16[4,128,1024]{2,1,0:T(8,128)(2,1)S(1)}, u32[]{:S(2)}, u32[]{:S(2)}) collective-permute-start(bf16[4,128,1024]{2,1,0:T(8,128)(2,1)S(1)} %all-to-all-done.5.mine_ref), channel_id=1, source_target_pairs={{0,16},{16,0},{1,17},{17,1},{2,18},{18,2},{3,19},{19,3},{4,20},{20... | collective-permute-start | bytes 3145736 | tf_op jit(solution)/shard_map/ppermute | solution.py:316
  127.7 4.1 %all-to-all-done.3.part_ref = bf16[4,512,128]{2,1,0:T(8,128)(2,1)S(1)} async-done(((bf16[4,512,128]{2,1,0:T(8,128)(2,1)}), bf16[4,512,128]{2,1,0:T(8,128)(2,1)S(1)}, u32[]{:S(2)}, u32[]{:S(2)}) %all-to-all-start.3) | async-done | bytes 524320 | tf_op jit(solution)/shard_map/all_to_all | solution.py:320
  131.8 0.9 key_grad.1
  132.7 8.9 %all-to-all-start.4 = ((bf16[8,64,512]{2,1,0:T(8,128)(2,1)}), bf16[8,64,512]{2,1,0:T(8,128)(2,1)S(1)}, u32[]{:S(2)}, u32[]{:S(2)}) async-start(bf16[8,64,512]{2,1,0:T(8,128)(2,1)} %bitcast.12), calls=%async_computation.4 | async-start | bytes 1048576 | tf_op jit(solution)/shard_map/all_to_all | solution.py:322
  141.6 0.0 collective-permute-done.4.other_ref
  141.6 9.1 %all-to-all-done.4 = bf16[8,64,512]{2,1,0:T(8,128)(2,1)S(1)} async-done(((bf16[8,64,512]{2,1,0:T(8,128)(2,1)}), bf16[8,64,512]{2,1,0:T(8,128)(2,1)S(1)}, u32[]{:S(2)}, u32[]{:S(2)}) %all-to-all-start.4) | async-done | bytes 524320 | tf_op jit(solution)/shard_map/all_to_all | solution.py:322
  150.6 0.7 project.1
  151.3 31.7 %all_to_all.35.part_ref = bf16[64,16,256]{2,1,0:T(8,128)(2,1)S(1)} all-to-all(bf16[64,16,256]{2,1,0:T(8,128)(2,1)S(1)} %bitcast.21), channel_id=1, replica_groups=mesh['yh'=4,'x'=4,'core'=2,'zh'=4,'zl'=2,'yl'=2] {'yh','x','zh'}, dimensions={0} | all-to-all | bytes 1048576 | tf_op jit(solution)/shard_map/all_to_all | solution.py:324
  183.1 0.2 total.1
  183.3 0.7 copy.9
  (2 shorter events, 0.0 us)
Async XLA Ops:
  0.0 8.5 %copy-start = (bf16[1,128,4096]{2,1,0:T(8,128)(2,1)S(1)}, bf16[1,128,4096]{2,1,0:T(8,128)(2,1)}, u32[]{:S(2)}) copy-start(bf16[1,128,4096]{2,1,0:T(8,128)(2,1)} %param.9) | copy-start | bytes 3145732
  0.7 0.9 copy-start.4
  1.6 0.9 copy-start.5
  3.3 9.6 %all-to-all-start.1 = ((bf16[4,2,128,128]{3,2,1,0:T(8,128)(2,1)}), bf16[4,2,128,128]{3,2,1,0:T(8,128)(2,1)S(1)}, u32[]{:S(2)}, u32[]{:S(2)}) async-start(bf16[4,2,128,128]{3,2,1,0:T(8,128)(2,1)} %pack_kv.1), calls=%async_computation.1 | async-start | bytes 524288 | tf_op jit(solution)/shard_map/all_to_all | solution.py:307
  8.5 1.2 copy-start.1
  9.7 0.7 copy-start.6
  10.5 0.7 copy-start.8
  12.9 3.8 %copy-start.2 = (bf16[1,128,4096]{2,1,0:T(8,128)(2,1)S(1)}, bf16[1,128,4096]{2,1,0:T(8,128)(2,1)}, u32[]{:S(2)}) copy-start(bf16[1,128,4096]{2,1,0:T(8,128)(2,1)} %param.10) | copy-start | bytes 3145732
  12.9 3.8 %copy-start.7 = (f32[1,128,32]{1,2,0:T(8,128)S(1)}, f32[1,128,32]{1,2,0:T(8,128)}, u32[]{:S(2)}) copy-start(f32[1,128,32]{1,2,0:T(8,128)} %param.13) | copy-start | bytes 49156
  12.9 3.8 %copy-start.9 = (f32[1,128,32]{1,2,0:T(8,128)S(1)}, f32[1,128,32]{1,2,0:T(8,128)}, u32[]{:S(2)}) copy-start(f32[1,128,32]{1,2,0:T(8,128)} %param.14) | copy-start | bytes 49156
  12.9 12.2 %all-to-all-start.2 = ((bf16[4,1056,128]{2,1,0:T(8,128)(2,1)}), bf16[4,1056,128]{2,1,0:T(8,128)(2,1)S(1)}, u32[]{:S(2)}, u32[]{:S(2)}) async-start(bf16[4,1056,128]{2,1,0:T(8,128)(2,1)} %pack_q0.1), calls=%async_computation.2 | async-start | bytes 2162688 | tf_op jit(solution)/shard_map/all_to_all | solution.py:310
  18.5 10.9 %copy-start.3 = (bf16[1,128,4096]{2,1,0:T(8,128)(2,1)S(1)}, bf16[1,128,4096]{2,1,0:T(8,128)(2,1)}, u32[]{:S(2)}) copy-start(bf16[1,128,4096]{2,1,0:T(8,128)(2,1)} %param.15) | copy-start | bytes 3145732
  25.2 12.8 %all-to-all-start = ((bf16[4,1056,128]{2,1,0:T(8,128)(2,1)}), bf16[4,1056,128]{2,1,0:T(8,128)(2,1)}, u32[]{:S(2)}, u32[]{:S(2)}) async-start(bf16[4,1056,128]{2,1,0:T(8,128)(2,1)} %pack_q1.1), calls=%async_computation | async-start | bytes 2162688 | tf_op jit(solution)/shard_map/all_to_all | solution.py:310
  37.9 62.0 %all-to-all-start.5 = ((bf16[4,128,1024]{2,1,0:T(8,128)(2,1)}), bf16[4,128,1024]{2,1,0:T(8,128)(2,1)S(1)}, u32[]{:S(2)}, u32[]{:S(2)}) async-start(bf16[4,128,1024]{2,1,0:T(8,128)(2,1)} %pack_x.1), calls=%async_computation.5 | async-start | bytes 2097152 | tf_op jit(solution)/shard_map/all_to_all | solution.py:315
  41.5 43.2 %collective-permute-start = (bf16[4,2,128,128]{3,2,1,0:T(8,128)(2,1)S(1)}, bf16[4,2,128,128]{3,2,1,0:T(8,128)(2,1)S(1)}, u32[]{:S(2)}, u32[]{:S(2)}) collective-permute-start(bf16[4,2,128,128]{3,2,1,0:T(8,128)(2,1)S(1)} %all-to-all-done.1.own_ref), channel_id=1, source_target_pairs={{0,4},{4,8},{8,12},{12,0},{1,5},{5,9},{9,13},{13,1},{2,6},{6,10},{... | collective-permute-start | bytes 786440 | tf_op jit(solution)/shard_map/ppermute | solution.py:299
  57.2 29.4 %collective-permute-start.1 = (bf16[4,2,128,128]{3,2,1,0:T(8,128)(2,1)S(1)}, bf16[4,2,128,128]{3,2,1,0:T(8,128)(2,1)S(1)}, u32[]{:S(2)}, u32[]{:S(2)}) collective-permute-start(bf16[4,2,128,128]{3,2,1,0:T(8,128)(2,1)S(1)} %all-to-all-done.1.own_ref), channel_id=1, source_target_pairs={{0,12},{4,0},{8,4},{12,8},{1,13},{5,1},{9,5},{13,9},{2,14},{6,2},{... | collective-permute-start | bytes 786440 | tf_op jit(solution)/shard_map/ppermute | solution.py:299
  84.7 7.8 %collective-permute-start.2 = (bf16[2,2,128,128]{3,2,1,0:T(8,128)(2,1)S(1)}, bf16[2,2,128,128]{3,2,1,0:T(8,128)(2,1)S(1)}, u32[]{:S(2)}, u32[]{:S(2)}) collective-permute-start(bf16[2,2,128,128]{3,2,1,0:T(8,128)(2,1)S(1)} %slice.8), channel_id=1, source_target_pairs={{0,4},{4,8},{8,12},{12,0},{1,5},{5,9},{9,13},{13,1},{2,6},{6,10},{... | collective-permute-start | bytes 393224 | tf_op jit(solution)/shard_map/ppermute | solution.py:299
  86.6 7.4 %collective-permute-start.3 = (bf16[2,2,128,128]{3,2,1,0:T(8,128)(2,1)S(1)}, bf16[2,2,128,128]{3,2,1,0:T(8,128)(2,1)S(1)}, u32[]{:S(2)}, u32[]{:S(2)}) collective-permute-start(bf16[2,2,128,128]{3,2,1,0:T(8,128)(2,1)S(1)} %slice.9), channel_id=1, source_target_pairs={{0,12},{4,0},{8,4},{12,8},{1,13},{5,1},{9,5},{13,9},{2,14},{6,2},{... | collective-permute-start | bytes 393224 | tf_op jit(solution)/shard_map/ppermute | solution.py:299
  100.0 31.8 %all-to-all-start.3 = ((bf16[4,512,128]{2,1,0:T(8,128)(2,1)}), bf16[4,512,128]{2,1,0:T(8,128)(2,1)S(1)}, u32[]{:S(2)}, u32[]{:S(2)}) async-start(bf16[4,512,128]{2,1,0:T(8,128)(2,1)} %convert_element_type.3), calls=%async_computation.3 | async-start | bytes 1048576 | tf_op jit(solution)/shard_map/all_to_all | solution.py:320
  122.4 19.2 %collective-permute-start.4 = (bf16[4,128,1024]{2,1,0:T(8,128)(2,1)S(1)}, bf16[4,128,1024]{2,1,0:T(8,128)(2,1)S(1)}, u32[]{:S(2)}, u32[]{:S(2)}) collective-permute-start(bf16[4,128,1024]{2,1,0:T(8,128)(2,1)S(1)} %all-to-all-done.5.mine_ref), channel_id=1, source_target_pairs={{0,16},{16,0},{1,17},{17,1},{2,18},{18,2},{3,19},{19,3},{4,20},{20... | collective-permute-start | bytes 3145736 | tf_op jit(solution)/shard_map/ppermute | solution.py:316
  132.7 17.9 %all-to-all-start.4 = ((bf16[8,64,512]{2,1,0:T(8,128)(2,1)}), bf16[8,64,512]{2,1,0:T(8,128)(2,1)S(1)}, u32[]{:S(2)}, u32[]{:S(2)}) async-start(bf16[8,64,512]{2,1,0:T(8,128)(2,1)} %bitcast.12), calls=%async_computation.4 | async-start | bytes 1048576 | tf_op jit(solution)/shard_map/all_to_all | solution.py:322

commit v2 on v1

v2 whole, which is shorter than its diff:
```python
import functools

import jax
import jax.numpy as jnp
import numpy as np
from jax import lax
from jax.experimental import pallas as pl
from jax.experimental.pallas import tpu as pltpu
from jax.sharding import Mesh, PartitionSpec as P

HQ = 32
KVH = 4
DH = 128
GROUP = HQ // KVH
CAP = 128
D = 4096
LOG2E = 1.4426950408889634
SCALE = DH ** (-0.5)
HOME = ("zl", "yl")
HALF = GROUP // 2
PACK_ROWS = 2 * GROUP * CAP + 8 * GROUP
SUPER = 4 * CAP
VMEM = 24 * 1024 * 1024
MOST_VMEM = 60 * 1024 * 1024


def split3(x):
    hi = x.astype(jnp.bfloat16)
    rest = x - hi.astype(jnp.float32)
    mid = rest.astype(jnp.bfloat16)
    lo = (rest - mid.astype(jnp.float32)).astype(jnp.bfloat16)
    return hi, mid, lo


def whole(*shape):
    return pl.BlockSpec(memory_space=pltpu.VMEM)


def pack_kv_kernel(count_ref, k_ref, v_ref, out_ref):
    rows = lax.broadcasted_iota(jnp.int32, (CAP, DH), 0)
    valid = rows < count_ref[0, 0]
    for g in range(KVH):
        cols = slice(g * DH, (g + 1) * DH)
        k = jnp.where(valid, k_ref[:, cols], jnp.zeros((), jnp.bfloat16))
        v = v_ref[:, cols]
        for z in range(4):
            out_ref[z, g, 0] = k
            out_ref[z, g, 1] = v


def pack_kv(counts, keys, values):
    return pl.pallas_call(
        pack_kv_kernel,
        out_shape=jax.ShapeDtypeStruct((4, KVH, 2, CAP, DH), jnp.bfloat16),
        in_specs=[pl.BlockSpec(memory_space=pltpu.SMEM), whole(), whole()],
        out_specs=whole(),
        compiler_params=pltpu.CompilerParams(vmem_limit_bytes=MOST_VMEM),
        name="pack_kv",
    )(counts, keys, values)


def pack_q_kernel(head_ref, count_ref, q_ref, d_ref, n_ref, t_ref, out_ref):
    for h in range(GROUP):
        cols = slice(h * DH, (h + 1) * DH)
        out_ref[h * CAP:(h + 1) * CAP] = q_ref[:, cols]
        out_ref[(GROUP + h) * CAP:(GROUP + h + 1) * CAP] = d_ref[:, cols]
    lane = lax.broadcasted_iota(jnp.int32, (GROUP, CAP), 1)
    norms = jnp.where(lane < count_ref[0], n_ref[...] * LOG2E, jnp.float32(1e30))
    parts = [*split3(norms), *split3(t_ref[...])]
    parts += [jnp.zeros((GROUP, CAP), jnp.bfloat16)] * 2
    out_ref[2 * GROUP * CAP:] = jnp.concatenate(
        [p.astype(jnp.float32) for p in parts], axis=0
    ).astype(jnp.bfloat16)


def pack_q(head, counts, query, grad, norms_t, dots_t):
    cols = lambda i, head, count: (0, head[0])
    rows = lambda i, head, count: (head[0], 0)
    return pl.pallas_call(
        pack_q_kernel,
        grid_spec=pltpu.PrefetchScalarGridSpec(
            num_scalar_prefetch=2,
            grid=(1,),
            in_specs=[
                pl.BlockSpec((CAP, GROUP * DH), cols),
                pl.BlockSpec((CAP, GROUP * DH), cols),
                pl.BlockSpec((GROUP, CAP), rows),
                pl.BlockSpec((GROUP, CAP), rows),
            ],
            out_specs=pl.BlockSpec((PACK_ROWS, DH), lambda i, head, count: (0, 0)),
        ),
        out_shape=jax.ShapeDtypeStruct((PACK_ROWS, DH), jnp.bfloat16),
        compiler_params=pltpu.CompilerParams(vmem_limit_bytes=VMEM),
        name="pack_q",
    )(head, counts.reshape(1), query, grad, norms_t, dots_t)


def pack_x_kernel(home_ref, count_ref, x_ref, *out_refs):
    rows = lax.broadcasted_iota(jnp.int32, (CAP, 256), 0)
    valid = rows < count_ref[0, 0]
    for flip, out_ref in enumerate(out_refs):
        for z in range(4):
            begin = pl.multiple_of(z * 1024 + (home_ref[0] ^ flip) * 256, 256)
            out_ref[:, z * 256:(z + 1) * 256] = jnp.where(
                valid, x_ref[:, pl.ds(begin, 256)], jnp.zeros((), jnp.bfloat16)
            )


def pack_x(home, counts, x):
    return pl.pallas_call(
        pack_x_kernel,
        out_shape=[jax.ShapeDtypeStruct((CAP, D // 4), jnp.bfloat16)] * 4,
        in_specs=[pl.BlockSpec(memory_space=pltpu.SMEM)] * 2 + [whole()],
        out_specs=[whole()] * 4,
        compiler_params=pltpu.CompilerParams(vmem_limit_bytes=VMEM),
        name="pack_x",
    )(home, counts, x)


def join_x_kernel(home_ref, *refs):
    for flip, ref in enumerate(refs[:-1]):
        refs[-1][home_ref[0] ^ flip] = ref[...]


def join_x(home, parts):
    return pl.pallas_call(
        join_x_kernel,
        out_shape=jax.ShapeDtypeStruct((4, CAP, D // 4), jnp.bfloat16),
        in_specs=[pl.BlockSpec(memory_space=pltpu.SMEM)] + [whole()] * 4,
        out_specs=whole(),
        compiler_params=pltpu.CompilerParams(vmem_limit_bytes=VMEM),
        name="join_x",
    )(home, *parts)


NT = (((1,), (1,)), ((), ()))
NN = (((1,), (0,)), ((), ()))


def attend(qd_ref, k, v, keep=None):
    q = qd_ref[0:GROUP * CAP]
    d = qd_ref[GROUP * CAP:2 * GROUP * CAP]
    small = qd_ref[2 * GROUP * CAP:].astype(jnp.float32)
    norm = small[0:8] + small[8:16] + small[16:24]
    dot = small[24:32] + small[32:40] + small[40:48]
    out = []
    for half in range(2):
        part = slice(half * HALF * CAP, (half + 1) * HALF * CAP)
        scores = lax.dot_general(k, q[part], NT, preferred_element_type=jnp.float32)
        dprobs = lax.dot_general(v, d[part], NT, preferred_element_type=jnp.float32)
        for i in range(HALF):
            cols = slice(i * CAP, (i + 1) * CAP)
            h = half * HALF + i
            p = jnp.exp2(scores[:, cols] * (SCALE * LOG2E) - norm[h:h + 1])
            if keep is not None:
                p = jnp.where(keep, p, 0.0)
            out.append((p * (dprobs[:, cols] - dot[h:h + 1])).astype(jnp.bfloat16))
    ds = jnp.concatenate(out, axis=1)
    return lax.dot_general(ds, q, NN, preferred_element_type=jnp.float32)


def far_kernel(count, place_ref, kv_ref, *rest):
    q_refs, out_ref = rest[:count], rest[-1]
    zh = place_ref[0]

    def earlier(at, carry):
        keys = pl.ds(4 * at, 4)
        k = kv_ref[keys, 0].reshape(SUPER, DH)
        v = kv_ref[keys, 1].reshape(SUPER, DH)
        for i, q_ref in enumerate(q_refs):
            term = attend(q_ref, k, v)
            if i > 0:
                term = term + out_ref[at]
            elif len(rest) > count + 1:
                term = term + rest[count][at]
            out_ref[at] = term.astype(out_ref.dtype)
        return carry

    def later(at, carry):
        out_ref[at] = jnp.zeros((SUPER, DH), out_ref.dtype)
        return carry

    lax.fori_loop(0, zh, earlier, 0)
    lax.fori_loop(zh, 4, later, 0)


def far_call(place, kv, queries, before=None, kind=jnp.float32):
    args = [place, kv, *queries] + ([] if before is None else [before])
    return pl.pallas_call(
        functools.partial(far_kernel, len(queries)),
        out_shape=jax.ShapeDtypeStruct((4, SUPER, DH), kind),
        in_specs=[pl.BlockSpec(memory_space=pltpu.SMEM)] + [whole()] * (len(args) - 1),
        out_specs=whole(),
        compiler_params=pltpu.CompilerParams(vmem_limit_bytes=VMEM),
        cost_estimate=pl.CostEstimate(flops=1, bytes_accessed=1, transcendentals=0),
        name="far_%d" % len(queries),
    )(*args)


def near_kernel(flips, place_ref, kv_ref, *rest):
    q_refs, out_ref = rest[:len(flips)], rest[-1]
    keys = pl.ds(4 * place_ref[0], 4)
    k = kv_ref[keys, 0].reshape(SUPER, DH)
    v = kv_ref[keys, 1].reshape(SUPER, DH)
    row = lax.broadcasted_iota(jnp.int32, (SUPER, CAP), 0)
    lane = lax.broadcasted_iota(jnp.int32, (SUPER, CAP), 1)
    for i, (flip, q_ref) in enumerate(zip(flips, q_refs)):
        term = attend(q_ref, k, v, row <= lane + CAP * (place_ref[1] ^ flip))
        if i > 0:
            term = term + out_ref[...]
        elif len(rest) > len(flips) + 1:
            term = term + rest[-2][...]
        out_ref[...] = term


def near_call(place, kv, flips, queries, before=None):
    args = [place, kv, *queries] + ([] if before is None else [before])
    return pl.pallas_call(
        functools.partial(near_kernel, flips),
        out_shape=jax.ShapeDtypeStruct((SUPER, DH), jnp.float32),
        in_specs=[pl.BlockSpec(memory_space=pltpu.SMEM)] + [whole()] * (len(args) - 1),
        out_specs=whole(),
        compiler_params=pltpu.CompilerParams(vmem_limit_bytes=VMEM),
        cost_estimate=pl.CostEstimate(flops=1, bytes_accessed=1, transcendentals=0),
        name="near_%d" % flips[0],
    )(*args)


def key_grad_kernel(part_ref, near_ref, out_ref):
    total = near_ref[...]
    for z in range(4):
        total = total + part_ref[z].astype(jnp.float32)
    grad = (total * SCALE).T.astype(jnp.bfloat16)
    for core in range(2):
        rows = [x * 32 + core * 16 for x in range(4)]
        piece = jnp.concatenate([grad[r:r + 16] for r in rows], axis=0)
        for j in range(4):
            out_ref[core, j] = piece


def key_grad_call(parts, near):
    return pl.pallas_call(
        key_grad_kernel,
        out_shape=jax.ShapeDtypeStruct((2, 4, 64, SUPER), jnp.bfloat16),
        in_specs=[whole()] * 2,
        out_specs=whole(),
        compiler_params=pltpu.CompilerParams(vmem_limit_bytes=VMEM),
        name="key_grad",
    )(parts, near)


def project_kernel(core_ref, grad_ref, *refs):
    out_ref = refs[-1]
    total = None
    for flip, x_ref in enumerate(refs[:-1]):
        grad = grad_ref[core_ref[0] ^ flip].reshape(256, SUPER)
        x = x_ref[...].reshape(SUPER, D // 4)
        term = lax.dot_general(grad, x, NN, preferred_element_type=jnp.float32)
        total = term if total is None else total + term
    total = total.astype(jnp.bfloat16)
    for c in range(16):
        for z in range(4):
            out_ref[c, z] = total[c * 16:(c + 1) * 16, z * 256:(z + 1) * 256]


def project(core, grads, features):
    return pl.pallas_call(
        project_kernel,
        out_shape=jax.ShapeDtypeStruct((16, 4, 16, 256), jnp.bfloat16),
        in_specs=[pl.BlockSpec(memory_space=pltpu.SMEM)] + [whole()] * 3,
        out_specs=whole(),
        compiler_params=pltpu.CompilerParams(vmem_limit_bytes=VMEM),
        name="project",
    )(core, grads, *features)


def total_kernel(part_ref, out_ref):
    def step(i, total):
        return total + part_ref[i].astype(jnp.float32)

    total = part_ref[0].astype(jnp.float32)
    for i in range(1, 64):
        total = step(i, total)
    out_ref[...] = total.T


def total_call(parts):
    return pl.pallas_call(
        total_kernel,
        out_shape=jax.ShapeDtypeStruct((256, 16), jnp.float32),
        in_specs=[whole()],
        out_specs=whole(),
        compiler_params=pltpu.CompilerParams(vmem_limit_bytes=VMEM),
        name="total",
    )(parts)


def body(query, grad_out, keys, values, log_norm, row_dots, block_input, route_index, counts):
    del route_index
    zh = lax.axis_index("zh").astype(jnp.int32)
    home = lax.axis_index(HOME).astype(jnp.int32)
    core = lax.axis_index("core").astype(jnp.int32)
    kv = pack_kv(counts, keys[0], values[0]).reshape(16, 2, CAP, DH)
    kv = lax.all_to_all(kv, ("zh",) + HOME, 0, 0)
    norms_t, dots_t = log_norm[0].T, row_dots[0].T

    def to_home(x, flip):
        if flip == 0:
            return x
        return lax.ppermute(x, HOME, [(i, i ^ flip) for i in range(4)])

    def queries(flip):
        head = (home ^ flip).reshape(1)
        return to_home(pack_q(head, counts, query[0], grad_out[0], norms_t, dots_t), flip)

    place = jnp.stack([zh, home])
    own, beside_y, beside_z, diagonal = (queries(flip) for flip in range(4))
    pieces = list(pack_x(home.reshape(1), counts, block_input[0]))
    pieces[1] = to_home(pieces[1], 1)
    kv, beside_y = lax.optimization_barrier((kv, beside_y))
    far = far_call(place, kv, [own, beside_y])
    near = near_call(place, kv, (0, 1), [own, beside_y])
    far, near, *pieces[2:] = lax.optimization_barrier((far, near, *pieces[2:]))
    pieces[2:] = to_home(pieces[2], 2), to_home(pieces[3], 3)
    far, near, beside_z, diagonal = lax.optimization_barrier((far, near, beside_z, diagonal))
    far = far_call(place, kv, [beside_z, diagonal], far, jnp.bfloat16)
    far, *pieces = lax.optimization_barrier((far, *pieces))
    parts = lax.all_to_all(far, "zh", 0, 0)
    mine = join_x(home.reshape(1), pieces)
    other = lax.ppermute(mine, "core", [(0, 1), (1, 0)])
    near = near_call(place, kv, (2, 3), [beside_z, diagonal], near)
    grads = key_grad_call(parts, near)
    grads = lax.all_to_all(grads.reshape(8, 64, SUPER), ("core",) + HOME, 0, 0)
    local = project(core.reshape(1), grads.reshape(2, 4, 64, SUPER), [mine, other])
    parts = lax.all_to_all(local.reshape(64, 16, 256), ("yh", "x", "zh"), 0, 0)
    return total_call(parts)


def solution(mesh):
    fine = Mesh(
        np.asarray(mesh.devices).reshape(4, 4, 2, 4, 2, 2), ("yh", "x", "core", "zh", "zl", "yl")
    )
    dp, ctx = ("yh", "x", "core"), ("zh", "zl", "yl")
    in_specs = (P(dp, ctx, None),) * 7 + (P(dp, ctx),) * 2
    return jax.shard_map(body, mesh=fine, in_specs=in_specs, out_specs=P(ctx, dp), check_vma=False)
```

time: 185 us -> 146 us (0.79)
  starting transfers between devices: 82.3 us -> 50.2 us
  waiting for transfers between devices: 50.7 us -> 36.7 us
  Pallas kernels: 12.3 us -> 19.5 us
    all_to_all x5 -> x2, starting transfers between devices: 39.1 us -> 17 us  [the longest x1 12.1 us: body(): kv = lax.all_to_all(kv, ('zh',) + HOME, 0, 0)]
    all_to_all x5 -> x2, waiting for transfers between devices: 18.2 us -> 0.01 us  [the longest x1 0.01 us: body(): kv = lax.all_to_all(kv, ('zh',) + HOME, 0, 0)]
    ppermute x4 -> x6, starting transfers between devices: 29 us -> 17.4 us  [to_home(): return lax.ppermute(x, HOME, [(i, i ^ flip) for i in range(4)])]
    pallas_call x6 -> x11, Pallas kernels: 10.4 us -> 16.4 us  [the longest x2 6.16 us: near_call(): pl.pallas_call(functools.partial(near_kernel, flips), out_shape=jax.Shape...]
    ppermute x4 -> x6, waiting for transfers between devices: 23.5 us -> 27.6 us  [to_home(): return lax.ppermute(x, HOME, [(i, i ^ flip) for i in range(4)])]
    all_to_all x1, starting transfers between devices: 8.85 us -> 11 us  [body(): grads = lax.all_to_all(grads.reshape(8, 64, SUPER), ('core',) + HOME, 0, 0)]
    unnamed x20 -> x26, local copies, waits for them, and re-layouts: 4.48 us -> 5.64 us
  transfers between devices with their start and end apart: 11 -> 10, of which waited for: 7 -> 4; matrix products, arithmetic and copies ran while one was open for 0% -> 0% of each run, Pallas kernels for 6% -> 11%
where the time goes in v2:
time: 146 us; the launch traced here: 145 us
  starting transfers between devices  50.2 us (34%)
  waiting for transfers between devices  36.7 us (25%)
  blocking collectives  31.5 us (22%)
  Pallas kernels  19.5 us (13%)
  local copies, waits for them, and re-layouts  6.31 us (4%)
    all_to_all x1, blocking collectives, body(): parts = lax.all_to_all(local.reshape(64, 16, 256), ('yh', 'x', 'zh'), 0, 0)  31.5 us
    ppermute x6, waiting for transfers between devices, to_home(): return lax.ppermute(x, HOME, [(i, i ^ flip) for i in range(4)])  27.6 us
    ppermute x6, starting transfers between devices, to_home(): return lax.ppermute(x, HOME, [(i, i ^ flip) for i in range(4)])  17.4 us
    all_to_all x1, starting transfers between devices, body(): kv = lax.all_to_all(kv, ('zh',) + HOME, 0, 0)  12.1 us
    all_to_all x1, starting transfers between devices, body(): grads = lax.all_to_all(grads.reshape(8, 64, SUPER), ('core',) + HOME, 0, 0)  11 us
    all_to_all x1, waiting for transfers between devices, body(): grads = lax.all_to_all(grads.reshape(8, 64, SUPER), ('core',) + HOME, 0, 0)  9.05 us
    pallas_call x2, Pallas kernels, near_call(): pl.pallas_call(functools.partial(near_kernel, flips), out_shape=jax.Shape...  6.16 us
    unnamed x26, local copies, waits for them, and re-layouts  5.64 us
  transfers between devices with their start and end apart: 10, of which 4 were waited for; matrix products, arithmetic and copies ran while one was open for 0% of the time, Pallas kernels for 11%

profile of v2, /device:TPU:1, one launch (start us, length us, event | category | flops | bytes accessed | tf_op | source)
XLA Modules:
  0.0 145.1 jit_solution(16370358181260547617)
XLA Ops:
  0.7 0.0 copy-start.6
  0.7 2.1 %pack_kv.1 = bf16[4,4,2,128,128]{4,3,2,1,0:T(8,128)(2,1)} custom-call(s32[1,1]{1,0:T(1,128)} %copy.10.count_ref, bf16[128,512]{1,0:T(8,128)(2,1)} %bitcast.46, bf16[128,512]{1,0:T(8,128)(2,1)} %bitcast.47), custom_call_target="tpu_custom_call" | custom-call | tf_op jit(solution)/shard_map/pack_kv/pallas_call | solution.py:52
  2.8 0.0 copy-start
  2.8 0.0 copy-start.1
  2.8 12.1 %all-to-all-start = ((bf16[16,2,128,128]{3,2,1,0:T(8,128)(2,1)}), bf16[16,2,128,128]{3,2,1,0:T(8,128)(2,1)S(1)}, u32[]{:S(2)}, u32[]{:S(2)}) async-start(bf16[16,2,128,128]{3,2,1,0:T(8,128)(2,1)} %bitcast.45), calls=%async_computation | async-start | bytes 2097152 | tf_op jit(solution)/shard_map/all_to_all | solution.py:304
  14.9 0.0 copy-start.5
  14.9 0.0 copy-done.6
  15.0 0.0 copy-done
  15.0 0.0 copy-done.1
  15.0 0.7 copy-done.5
  15.6 0.9 pack_q.4
  16.6 3.3 %collective-permute-start = (bf16[2112,128]{1,0:T(8,128)(2,1)}, bf16[2112,128]{1,0:T(8,128)(2,1)}, u32[]{:S(2)}, u32[]{:S(2)}) collective-permute-start(bf16[2112,128]{1,0:T(8,128)(2,1)} %pack_q.4), channel_id=1, source_target_pairs={{0,1},{1,0},{2,3},{3,2},{4,5},{5,4},{6,7},{7,6},{8,9},{9,8},{10,11... | collective-permute-start | bytes 1622024 | tf_op jit(solution)/shard_map/ppermute | solution.py:310
  19.9 0.9 pack_q.6
  20.8 3.1 %collective-permute-start.1 = (bf16[2112,128]{1,0:T(8,128)(2,1)}, bf16[2112,128]{1,0:T(8,128)(2,1)}, u32[]{:S(2)}, u32[]{:S(2)}) collective-permute-start(bf16[2112,128]{1,0:T(8,128)(2,1)} %pack_q.6), channel_id=1, source_target_pairs={{0,2},{1,3},{2,0},{3,1},{4,6},{5,7},{6,4},{7,5},{8,10},{9,11},{10,... | collective-permute-start | bytes 1622024 | tf_op jit(solution)/shard_map/ppermute | solution.py:310
  23.9 0.0 copy-start.4
  23.9 0.9 pack_q.7
  24.8 2.0 %collective-permute-start.2 = (bf16[2112,128]{1,0:T(8,128)(2,1)}, bf16[2112,128]{1,0:T(8,128)(2,1)}, u32[]{:S(2)}, u32[]{:S(2)}) collective-permute-start(bf16[2112,128]{1,0:T(8,128)(2,1)} %pack_q.7), channel_id=1, source_target_pairs={{0,3},{1,2},{2,1},{3,0},{4,7},{5,6},{6,5},{7,4},{8,11},{9,10},{10,... | collective-permute-start | bytes 1622024 | tf_op jit(solution)/shard_map/ppermute | solution.py:310
  26.8 0.0 copy-done.4
  26.9 0.9 pack_x.1
  27.7 0.0 copy-start.9
  27.7 0.7 copy-done.9
  28.4 0.0 copy-start.11
  28.4 0.7 copy-done.11
  29.1 3.3 %collective-permute-start.3 = (bf16[128,1024]{1,0:T(8,128)(2,1)}, bf16[128,1024]{1,0:T(8,128)(2,1)}, u32[]{:S(2)}, u32[]{:S(2)}) collective-permute-start(bf16[128,1024]{1,0:T(8,128)(2,1)} %get-tuple-element.34), channel_id=1, source_target_pairs={{0,1},{1,0},{2,3},{3,2},{4,5},{5,4},{6,7},{7,6},{8,9},{9,8},{10,11... | collective-permute-start | bytes 786440 | tf_op jit(solution)/shard_map/ppermute | solution.py:310
  32.4 0.1 pack_q.5.rest_0_
  32.6 0.0 copy-start.2
  32.6 0.8 copy-done.2
  33.4 0.1 pad_add_fusion.place_ref
  33.4 10.0 %collective-permute-done.rest_1_ = bf16[2112,128]{1,0:T(8,128)(2,1)} collective-permute-done((bf16[2112,128]{1,0:T(8,128)(2,1)}, bf16[2112,128]{1,0:T(8,128)(2,1)}, u32[]{:S(2)}, u32[]{:S(2)}) %collective-permute-start) | collective-permute-done | bytes 540704 | tf_op jit(solution)/shard_map/ppermute | solution.py:310
  43.4 0.0 all-to-all-done.kv_ref
  43.4 0.0 copy-start.3
  43.4 1.0 copy-done.3
  44.5 3.0 %near_0.1.rest_2_ = f32[512,128]{1,0:T(8,128)S(1)} custom-call(s32[2]{0:T(128)S(1)} %pad_add_fusion.place_ref, bf16[16,2,128,128]{3,2,1,0:T(8,128)(2,1)S(1)} %all-to-all-done.kv_ref, bf16[2112,128]{1,0:T(8,128)(2,1)S(1)} %copy-done.3, bf16[2112,128]{1,0:T(8,128)(2,1)} %collective-permute-done.rest_1_), custom_call_target="tpu_custom_call" | custom-call | flops 1 | bytes 1 | tf_op jit(solution)/shard_map/near_0/pallas_call | solution.py:218
  47.5 0.0 copy-start.12
  47.5 0.0 copy-start.10
  47.5 1.2 far_2.2.rest_2_
  48.7 0.0 copy-done.12
  48.7 3.9 %collective-permute-start.4 = (bf16[128,1024]{1,0:T(8,128)(2,1)S(1)}, bf16[128,1024]{1,0:T(8,128)(2,1)S(1)}, u32[]{:S(2)}, u32[]{:S(2)}) collective-permute-start(bf16[128,1024]{1,0:T(8,128)(2,1)S(1)} %copy-done.12), channel_id=1, source_target_pairs={{0,2},{1,3},{2,0},{3,1},{4,6},{5,7},{6,4},{7,5},{8,10},{9,11},{10,... | collective-permute-start | bytes 786440 | tf_op jit(solution)/shard_map/ppermute | solution.py:310
  52.6 0.0 copy-done.10
  52.6 1.9 %collective-permute-start.5 = (bf16[128,1024]{1,0:T(8,128)(2,1)S(1)}, bf16[128,1024]{1,0:T(8,128)(2,1)S(1)}, u32[]{:S(2)}, u32[]{:S(2)}) collective-permute-start(bf16[128,1024]{1,0:T(8,128)(2,1)S(1)} %copy-done.10), channel_id=1, source_target_pairs={{0,3},{1,2},{2,1},{3,0},{4,7},{5,6},{6,5},{7,4},{8,11},{9,10},{10,... | collective-permute-start | bytes 786440 | tf_op jit(solution)/shard_map/ppermute | solution.py:310
  54.5 9.5 %collective-permute-done.1.rest_0_ = bf16[2112,128]{1,0:T(8,128)(2,1)} collective-permute-done((bf16[2112,128]{1,0:T(8,128)(2,1)}, bf16[2112,128]{1,0:T(8,128)(2,1)}, u32[]{:S(2)}, u32[]{:S(2)}) %collective-permute-start.1) | collective-permute-done | bytes 540704 | tf_op jit(solution)/shard_map/ppermute | solution.py:310
  64.0 0.0 collective-permute-done.2.rest_1_
  64.0 2.1 %far_2.3 = bf16[4,512,128]{2,1,0:T(8,128)(2,1)} custom-call(s32[2]{0:T(128)S(1)} %pad_add_fusion.place_ref, bf16[16,2,128,128]{3,2,1,0:T(8,128)(2,1)S(1)} %all-to-all-done.kv_ref, bf16[2112,128]{1,0:T(8,128)(2,1)} %collective-permute-done.1.rest_0_, bf16[2112,128]{1,0:T(8,128)(2,1)} %collective-permute-done.2.rest_1_, f32[4,512,128]{2,1,0:T(8,128)S(1)} %far_2.2.rest_2_), custom_call_target="tpu_custom_call" | custom-call | flops 1 | bytes 1 | tf_op jit(solution)/shard_map/far_2/pallas_call | solution.py:189
  66.1 0.0 collective-permute-done.3.refs_1_
  66.1 8.2 %collective-permute-done.4.refs_2_ = bf16[128,1024]{1,0:T(8,128)(2,1)S(1)} collective-permute-done((bf16[128,1024]{1,0:T(8,128)(2,1)S(1)}, bf16[128,1024]{1,0:T(8,128)(2,1)S(1)}, u32[]{:S(2)}, u32[]{:S(2)}) %collective-permute-start.4) | collective-permute-done | bytes 262176 | tf_op jit(solution)/shard_map/ppermute | solution.py:310
  74.3 0.0 collective-permute-done.5.refs_3_
  74.3 0.0 copy-start.7
  74.3 0.7 copy-done.7
  75.0 4.9 %all-to-all-start.1 = ((bf16[4,512,128]{2,1,0:T(8,128)(2,1)}), bf16[4,512,128]{2,1,0:T(8,128)(2,1)S(1)}, u32[]{:S(2)}, u32[]{:S(2)}) async-start(bf16[4,512,128]{2,1,0:T(8,128)(2,1)} %far_2.3), calls=%async_computation.1 | async-start | bytes 1048576 | tf_op jit(solution)/shard_map/all_to_all | solution.py:328
  79.9 0.0 copy-start.8
  79.9 0.9 copy-done.8
  80.9 1.0 join_x.1.refs_0_
  81.9 4.7 %collective-permute-start.6 = (bf16[4,128,1024]{2,1,0:T(8,128)(2,1)S(1)}, bf16[4,128,1024]{2,1,0:T(8,128)(2,1)}, u32[]{:S(2)}, u32[]{:S(2)}) collective-permute-start(bf16[4,128,1024]{2,1,0:T(8,128)(2,1)S(1)} %join_x.1.refs_0_), channel_id=1, source_target_pairs={{0,16},{16,0},{1,17},{17,1},{2,18},{18,2},{3,19},{19,3},{4,20},{20... | collective-permute-start | bytes 3145736 | tf_op jit(solution)/shard_map/ppermute | solution.py:330
  86.6 3.2 %near_2.1.near_ref = f32[512,128]{1,0:T(8,128)S(1)} custom-call(s32[2]{0:T(128)S(1)} %pad_add_fusion.place_ref, bf16[16,2,128,128]{3,2,1,0:T(8,128)(2,1)S(1)} %all-to-all-done.kv_ref, bf16[2112,128]{1,0:T(8,128)(2,1)} %collective-permute-done.1.rest_0_, bf16[2112,128]{1,0:T(8,128)(2,1)} %collective-permute-done.2.rest_1_, f32[512,128]{1,0:T(8,128)S(1)} %near_0.1.rest_2_), custom_call_target="tpu_custom_call" | custom-call | flops 1 | bytes 1 | tf_op jit(solution)/shard_map/near_2/pallas_call | solution.py:218
  89.8 0.0 all-to-all-done.1.part_ref
  89.8 1.0 key_grad.1
  90.8 11.0 %all-to-all-start.2 = ((bf16[8,64,512]{2,1,0:T(8,128)(2,1)}), bf16[8,64,512]{2,1,0:T(8,128)(2,1)S(1)}, u32[]{:S(2)}, u32[]{:S(2)}) async-start(bf16[8,64,512]{2,1,0:T(8,128)(2,1)} %bitcast.19), calls=%async_computation.2 | async-start | bytes 1048576 | tf_op jit(solution)/shard_map/all_to_all | solution.py:333
  101.8 0.0 collective-permute-done.6.refs_1_
  101.8 9.1 %all-to-all-done.2 = bf16[8,64,512]{2,1,0:T(8,128)(2,1)S(1)} async-done(((bf16[8,64,512]{2,1,0:T(8,128)(2,1)}), bf16[8,64,512]{2,1,0:T(8,128)(2,1)S(1)}, u32[]{:S(2)}, u32[]{:S(2)}) %all-to-all-start.2) | async-done | bytes 524320 | tf_op jit(solution)/shard_map/all_to_all | solution.py:333
  110.9 1.9 %project.1 = bf16[16,4,16,256]{3,2,1,0:T(8,128)(2,1)S(1)} custom-call(s32[1]{0:T(128)} %bitcast.core_ref, bf16[2,4,64,512]{3,2,1,0:T(8,128)(2,1)S(1)} %bitcast.34, bf16[4,128,1024]{2,1,0:T(8,128)(2,1)S(1)} %join_x.1.refs_0_, bf16[4,128,1024]{2,1,0:T(8,128)(2,1)} %collective-permute-done.6.refs_1_), custom_call_target="tpu_custom_call" | custom-call | tf_op jit(solution)/shard_map/project/pallas_call | solution.py:267
  112.8 31.5 %all_to_all.20.part_ref = bf16[64,16,256]{2,1,0:T(8,128)(2,1)S(1)} all-to-all(bf16[64,16,256]{2,1,0:T(8,128)(2,1)S(1)} %bitcast.35), channel_id=1, replica_groups=mesh['yh'=4,'x'=4,'core'=2,'zh'=4,'zl'=2,'yl'=2] {'yh','x','zh'}, dimensions={0} | all-to-all | bytes 1048576 | tf_op jit(solution)/shard_map/all_to_all | solution.py:335
  144.3 0.2 total.1
  144.5 0.7 copy.9
Async XLA Ops:
  0.7 14.3 %copy-start.6 = (f32[1,128,32]{1,2,0:T(8,128)S(1)}, f32[1,128,32]{1,2,0:T(8,128)}, u32[]{:S(2)}) copy-start(f32[1,128,32]{1,2,0:T(8,128)} %param.14) | copy-start | bytes 49156
  2.8 12.2 %copy-start = (bf16[1,128,4096]{2,1,0:T(8,128)(2,1)S(1)}, bf16[1,128,4096]{2,1,0:T(8,128)(2,1)}, u32[]{:S(2)}) copy-start(bf16[1,128,4096]{2,1,0:T(8,128)(2,1)} %param.9) | copy-start | bytes 3145732
  2.8 12.2 %copy-start.1 = (bf16[1,128,4096]{2,1,0:T(8,128)(2,1)S(1)}, bf16[1,128,4096]{2,1,0:T(8,128)(2,1)}, u32[]{:S(2)}) copy-start(bf16[1,128,4096]{2,1,0:T(8,128)(2,1)} %param.10) | copy-start | bytes 3145732
  2.8 40.6 %all-to-all-start = ((bf16[16,2,128,128]{3,2,1,0:T(8,128)(2,1)}), bf16[16,2,128,128]{3,2,1,0:T(8,128)(2,1)S(1)}, u32[]{:S(2)}, u32[]{:S(2)}) async-start(bf16[16,2,128,128]{3,2,1,0:T(8,128)(2,1)} %bitcast.45), calls=%async_computation | async-start | bytes 2097152 | tf_op jit(solution)/shard_map/all_to_all | solution.py:304
  14.9 0.7 copy-start.5
  16.6 26.8 %collective-permute-start = (bf16[2112,128]{1,0:T(8,128)(2,1)}, bf16[2112,128]{1,0:T(8,128)(2,1)}, u32[]{:S(2)}, u32[]{:S(2)}) collective-permute-start(bf16[2112,128]{1,0:T(8,128)(2,1)} %pack_q.4), channel_id=1, source_target_pairs={{0,1},{1,0},{2,3},{3,2},{4,5},{5,4},{6,7},{7,6},{8,9},{9,8},{10,11... | collective-permute-start | bytes 1622024 | tf_op jit(solution)/shard_map/ppermute | solution.py:310
  20.8 43.2 %collective-permute-start.1 = (bf16[2112,128]{1,0:T(8,128)(2,1)}, bf16[2112,128]{1,0:T(8,128)(2,1)}, u32[]{:S(2)}, u32[]{:S(2)}) collective-permute-start(bf16[2112,128]{1,0:T(8,128)(2,1)} %pack_q.6), channel_id=1, source_target_pairs={{0,2},{1,3},{2,0},{3,1},{4,6},{5,7},{6,4},{7,5},{8,10},{9,11},{10,... | collective-permute-start | bytes 1622024 | tf_op jit(solution)/shard_map/ppermute | solution.py:310
  23.9 2.9 %copy-start.4 = (bf16[1,128,4096]{2,1,0:T(8,128)(2,1)S(1)}, bf16[1,128,4096]{2,1,0:T(8,128)(2,1)}, u32[]{:S(2)}) copy-start(bf16[1,128,4096]{2,1,0:T(8,128)(2,1)} %param.15) | copy-start | bytes 3145732
  24.8 39.2 %collective-permute-start.2 = (bf16[2112,128]{1,0:T(8,128)(2,1)}, bf16[2112,128]{1,0:T(8,128)(2,1)}, u32[]{:S(2)}, u32[]{:S(2)}) collective-permute-start(bf16[2112,128]{1,0:T(8,128)(2,1)} %pack_q.7), channel_id=1, source_target_pairs={{0,3},{1,2},{2,1},{3,0},{4,7},{5,6},{6,5},{7,4},{8,11},{9,10},{10,... | collective-permute-start | bytes 1622024 | tf_op jit(solution)/shard_map/ppermute | solution.py:310
  27.7 0.7 copy-start.9
  28.4 0.7 copy-start.11
  29.1 37.0 %collective-permute-start.3 = (bf16[128,1024]{1,0:T(8,128)(2,1)}, bf16[128,1024]{1,0:T(8,128)(2,1)}, u32[]{:S(2)}, u32[]{:S(2)}) collective-permute-start(bf16[128,1024]{1,0:T(8,128)(2,1)} %get-tuple-element.34), channel_id=1, source_target_pairs={{0,1},{1,0},{2,3},{3,2},{4,5},{5,4},{6,7},{7,6},{8,9},{9,8},{10,11... | collective-permute-start | bytes 786440 | tf_op jit(solution)/shard_map/ppermute | solution.py:310
  32.6 0.8 copy-start.2
  43.4 1.0 copy-start.3
  47.5 1.2 copy-start.12
  47.5 5.1 %copy-start.10 = (bf16[128,1024]{1,0:T(8,128)(2,1)S(1)}, bf16[128,1024]{1,0:T(8,128)(2,1)}, u32[]{:S(2)}) copy-start(bf16[128,1024]{1,0:T(8,128)(2,1)} %copy-done.9) | copy-start | bytes 786436
  48.7 25.6 %collective-permute-start.4 = (bf16[128,1024]{1,0:T(8,128)(2,1)S(1)}, bf16[128,1024]{1,0:T(8,128)(2,1)S(1)}, u32[]{:S(2)}, u32[]{:S(2)}) collective-permute-start(bf16[128,1024]{1,0:T(8,128)(2,1)S(1)} %copy-done.12), channel_id=1, source_target_pairs={{0,2},{1,3},{2,0},{3,1},{4,6},{5,7},{6,4},{7,5},{8,10},{9,11},{10,... | collective-permute-start | bytes 786440 | tf_op jit(solution)/shard_map/ppermute | solution.py:310
  52.6 21.7 %collective-permute-start.5 = (bf16[128,1024]{1,0:T(8,128)(2,1)S(1)}, bf16[128,1024]{1,0:T(8,128)(2,1)S(1)}, u32[]{:S(2)}, u32[]{:S(2)}) collective-permute-start(bf16[128,1024]{1,0:T(8,128)(2,1)S(1)} %copy-done.10), channel_id=1, source_target_pairs={{0,3},{1,2},{2,1},{3,0},{4,7},{5,6},{6,5},{7,4},{8,11},{9,10},{10,... | collective-permute-start | bytes 786440 | tf_op jit(solution)/shard_map/ppermute | solution.py:310
  74.3 0.7 copy-start.7
  75.0 14.8 %all-to-all-start.1 = ((bf16[4,512,128]{2,1,0:T(8,128)(2,1)}), bf16[4,512,128]{2,1,0:T(8,128)(2,1)S(1)}, u32[]{:S(2)}, u32[]{:S(2)}) async-start(bf16[4,512,128]{2,1,0:T(8,128)(2,1)} %far_2.3), calls=%async_computation.1 | async-start | bytes 1048576 | tf_op jit(solution)/shard_map/all_to_all | solution.py:328
  79.9 0.9 copy-start.8
  81.9 19.9 %collective-permute-start.6 = (bf16[4,128,1024]{2,1,0:T(8,128)(2,1)S(1)}, bf16[4,128,1024]{2,1,0:T(8,128)(2,1)}, u32[]{:S(2)}, u32[]{:S(2)}) collective-permute-start(bf16[4,128,1024]{2,1,0:T(8,128)(2,1)S(1)} %join_x.1.refs_0_), channel_id=1, source_target_pairs={{0,16},{16,0},{1,17},{17,1},{2,18},{18,2},{3,19},{19,3},{4,20},{20... | collective-permute-start | bytes 3145736 | tf_op jit(solution)/shard_map/ppermute | solution.py:330
  90.8 20.1 %all-to-all-start.2 = ((bf16[8,64,512]{2,1,0:T(8,128)(2,1)}), bf16[8,64,512]{2,1,0:T(8,128)(2,1)S(1)}, u32[]{:S(2)}, u32[]{:S(2)}) async-start(bf16[8,64,512]{2,1,0:T(8,128)(2,1)} %bitcast.19), calls=%async_computation.2 | async-start | bytes 1048576 | tf_op jit(solution)/shard_map/all_to_all | solution.py:333

commit v3 on v2

--- a/solution.py
+++ b/solution.py
@@ -281,13 +281,13 @@
     total = part_ref[0].astype(jnp.float32)
     for i in range(1, 64):
         total = step(i, total)
-    out_ref[...] = total.T
+    out_ref[...] = total
 
 
 def total_call(parts):
     return pl.pallas_call(
         total_kernel,
-        out_shape=jax.ShapeDtypeStruct((256, 16), jnp.float32),
+        out_shape=jax.ShapeDtypeStruct((16, 256), jnp.float32),
         in_specs=[whole()],
         out_specs=whole(),
         compiler_params=pltpu.CompilerParams(vmem_limit_bytes=VMEM),
@@ -333,7 +333,7 @@
     grads = lax.all_to_all(grads.reshape(8, 64, SUPER), ("core",) + HOME, 0, 0)
     local = project(core.reshape(1), grads.reshape(2, 4, 64, SUPER), [mine, other])
     parts = lax.all_to_all(local.reshape(64, 16, 256), ("yh", "x", "zh"), 0, 0)
-    return total_call(parts)
+    return total_call(parts).T
 
 
 def solution(mesh):

time: 146 us -> 146 us (level)
  no operation moved by 1% of the time
where the time goes in v3:
time: 146 us; the launch traced here: 145 us
  starting transfers between devices  50.2 us (34%)
  waiting for transfers between devices  36.7 us (25%)
  blocking collectives  31.5 us (22%)
  Pallas kernels  20.1 us (14%)
  local copies, waits for them, and re-layouts  5.64 us (4%)
    all_to_all x1, blocking collectives, body(): parts = lax.all_to_all(local.reshape(64, 16, 256), ('yh', 'x', 'zh'), 0, 0)  31.5 us
    ppermute x6, waiting for transfers between devices, to_home(): return lax.ppermute(x, HOME, [(i, i ^ flip) for i in range(4)])  27.6 us
    ppermute x6, starting transfers between devices, to_home(): return lax.ppermute(x, HOME, [(i, i ^ flip) for i in range(4)])  17.4 us
    all_to_all x1, starting transfers between devices, body(): kv = lax.all_to_all(kv, ('zh',) + HOME, 0, 0)  12.1 us
    all_to_all x1, starting transfers between devices, body(): grads = lax.all_to_all(grads.reshape(8, 64, SUPER), ('core',) + HOME, 0, 0)  11 us
    all_to_all x1, waiting for transfers between devices, body(): grads = lax.all_to_all(grads.reshape(8, 64, SUPER), ('core',) + HOME, 0, 0)  9.05 us
    pallas_call x2, Pallas kernels, near_call(): pl.pallas_call(functools.partial(near_kernel, flips), out_shape=jax.Shape...  6.16 us
    unnamed x26, local copies, waits for them, and re-layouts  5.64 us
  transfers between devices with their start and end apart: 10, of which 4 were waited for; matrix products, arithmetic and copies ran while one was open for 0% of the time, Pallas kernels for 11%

profile of v3, /device:TPU:1, one launch (start us, length us, event | category | flops | bytes accessed | tf_op | source)
XLA Modules:
  0.0 145.0 jit_solution(4507671206725350188)
XLA Ops:
  0.7 0.0 copy-start.6
  0.7 2.1 %pack_kv.1 = bf16[4,4,2,128,128]{4,3,2,1,0:T(8,128)(2,1)} custom-call(s32[1,1]{1,0:T(1,128)} %copy.9.count_ref, bf16[128,512]{1,0:T(8,128)(2,1)} %bitcast.47, bf16[128,512]{1,0:T(8,128)(2,1)} %bitcast.48), custom_call_target="tpu_custom_call" | custom-call | tf_op jit(solution)/shard_map/pack_kv/pallas_call | solution.py:52
  2.8 0.0 copy-start
  2.8 0.0 copy-start.1
  2.8 12.1 %all-to-all-start = ((bf16[16,2,128,128]{3,2,1,0:T(8,128)(2,1)}), bf16[16,2,128,128]{3,2,1,0:T(8,128)(2,1)S(1)}, u32[]{:S(2)}, u32[]{:S(2)}) async-start(bf16[16,2,128,128]{3,2,1,0:T(8,128)(2,1)} %bitcast.46), calls=%async_computation | async-start | bytes 2097152 | tf_op jit(solution)/shard_map/all_to_all | solution.py:304
  14.9 0.0 copy-start.5
  14.9 0.0 copy-done.6
  15.0 0.0 copy-done
  15.0 0.0 copy-done.1
  15.0 0.7 copy-done.5
  15.6 0.9 pack_q.4
  16.6 3.3 %collective-permute-start = (bf16[2112,128]{1,0:T(8,128)(2,1)}, bf16[2112,128]{1,0:T(8,128)(2,1)}, u32[]{:S(2)}, u32[]{:S(2)}) collective-permute-start(bf16[2112,128]{1,0:T(8,128)(2,1)} %pack_q.4), channel_id=1, source_target_pairs={{0,1},{1,0},{2,3},{3,2},{4,5},{5,4},{6,7},{7,6},{8,9},{9,8},{10,11... | collective-permute-start | bytes 1622024 | tf_op jit(solution)/shard_map/ppermute | solution.py:310
  19.9 0.9 pack_q.6
  20.8 3.1 %collective-permute-start.1 = (bf16[2112,128]{1,0:T(8,128)(2,1)}, bf16[2112,128]{1,0:T(8,128)(2,1)}, u32[]{:S(2)}, u32[]{:S(2)}) collective-permute-start(bf16[2112,128]{1,0:T(8,128)(2,1)} %pack_q.6), channel_id=1, source_target_pairs={{0,2},{1,3},{2,0},{3,1},{4,6},{5,7},{6,4},{7,5},{8,10},{9,11},{10,... | collective-permute-start | bytes 1622024 | tf_op jit(solution)/shard_map/ppermute | solution.py:310
  23.9 0.0 copy-start.4
  23.9 0.9 pack_q.7
  24.8 2.0 %collective-permute-start.2 = (bf16[2112,128]{1,0:T(8,128)(2,1)}, bf16[2112,128]{1,0:T(8,128)(2,1)}, u32[]{:S(2)}, u32[]{:S(2)}) collective-permute-start(bf16[2112,128]{1,0:T(8,128)(2,1)} %pack_q.7), channel_id=1, source_target_pairs={{0,3},{1,2},{2,1},{3,0},{4,7},{5,6},{6,5},{7,4},{8,11},{9,10},{10,... | collective-permute-start | bytes 1622024 | tf_op jit(solution)/shard_map/ppermute | solution.py:310
  26.8 0.0 copy-done.4
  26.9 0.9 pack_x.1
  27.7 0.0 copy-start.9
  27.7 0.7 copy-done.9
  28.4 0.0 copy-start.11
  28.4 0.7 copy-done.11
  29.1 3.3 %collective-permute-start.3 = (bf16[128,1024]{1,0:T(8,128)(2,1)}, bf16[128,1024]{1,0:T(8,128)(2,1)}, u32[]{:S(2)}, u32[]{:S(2)}) collective-permute-start(bf16[128,1024]{1,0:T(8,128)(2,1)} %get-tuple-element.34), channel_id=1, source_target_pairs={{0,1},{1,0},{2,3},{3,2},{4,5},{5,4},{6,7},{7,6},{8,9},{9,8},{10,11... | collective-permute-start | bytes 786440 | tf_op jit(solution)/shard_map/ppermute | solution.py:310
  32.4 0.1 pack_q.5.rest_0_
  32.6 0.0 copy-start.2
  32.6 0.8 copy-done.2
  33.4 0.1 pad_add_fusion.place_ref
  33.4 10.0 %collective-permute-done.rest_1_ = bf16[2112,128]{1,0:T(8,128)(2,1)} collective-permute-done((bf16[2112,128]{1,0:T(8,128)(2,1)}, bf16[2112,128]{1,0:T(8,128)(2,1)}, u32[]{:S(2)}, u32[]{:S(2)}) %collective-permute-start) | collective-permute-done | bytes 540704 | tf_op jit(solution)/shard_map/ppermute | solution.py:310
  43.4 0.0 all-to-all-done.kv_ref
  43.4 0.0 copy-start.3
  43.4 1.0 copy-done.3
  44.5 3.0 %near_0.1.rest_2_ = f32[512,128]{1,0:T(8,128)S(1)} custom-call(s32[2]{0:T(128)S(1)} %pad_add_fusion.place_ref, bf16[16,2,128,128]{3,2,1,0:T(8,128)(2,1)S(1)} %all-to-all-done.kv_ref, bf16[2112,128]{1,0:T(8,128)(2,1)S(1)} %copy-done.3, bf16[2112,128]{1,0:T(8,128)(2,1)} %collective-permute-done.rest_1_), custom_call_target="tpu_custom_call" | custom-call | flops 1 | bytes 1 | tf_op jit(solution)/shard_map/near_0/pallas_call | solution.py:218
  47.5 0.0 copy-start.12
  47.5 0.0 copy-start.10
  47.5 1.2 far_2.2.rest_2_
  48.7 0.0 copy-done.12
  48.7 3.9 %collective-permute-start.4 = (bf16[128,1024]{1,0:T(8,128)(2,1)S(1)}, bf16[128,1024]{1,0:T(8,128)(2,1)S(1)}, u32[]{:S(2)}, u32[]{:S(2)}) collective-permute-start(bf16[128,1024]{1,0:T(8,128)(2,1)S(1)} %copy-done.12), channel_id=1, source_target_pairs={{0,2},{1,3},{2,0},{3,1},{4,6},{5,7},{6,4},{7,5},{8,10},{9,11},{10,... | collective-permute-start | bytes 786440 | tf_op jit(solution)/shard_map/ppermute | solution.py:310
  52.6 0.0 copy-done.10
  52.6 1.9 %collective-permute-start.5 = (bf16[128,1024]{1,0:T(8,128)(2,1)S(1)}, bf16[128,1024]{1,0:T(8,128)(2,1)S(1)}, u32[]{:S(2)}, u32[]{:S(2)}) collective-permute-start(bf16[128,1024]{1,0:T(8,128)(2,1)S(1)} %copy-done.10), channel_id=1, source_target_pairs={{0,3},{1,2},{2,1},{3,0},{4,7},{5,6},{6,5},{7,4},{8,11},{9,10},{10,... | collective-permute-start | bytes 786440 | tf_op jit(solution)/shard_map/ppermute | solution.py:310
  54.5 9.5 %collective-permute-done.1.rest_0_ = bf16[2112,128]{1,0:T(8,128)(2,1)} collective-permute-done((bf16[2112,128]{1,0:T(8,128)(2,1)}, bf16[2112,128]{1,0:T(8,128)(2,1)}, u32[]{:S(2)}, u32[]{:S(2)}) %collective-permute-start.1) | collective-permute-done | bytes 540704 | tf_op jit(solution)/shard_map/ppermute | solution.py:310
  64.0 0.0 collective-permute-done.2.rest_1_
  64.0 2.1 %far_2.3 = bf16[4,512,128]{2,1,0:T(8,128)(2,1)} custom-call(s32[2]{0:T(128)S(1)} %pad_add_fusion.place_ref, bf16[16,2,128,128]{3,2,1,0:T(8,128)(2,1)S(1)} %all-to-all-done.kv_ref, bf16[2112,128]{1,0:T(8,128)(2,1)} %collective-permute-done.1.rest_0_, bf16[2112,128]{1,0:T(8,128)(2,1)} %collective-permute-done.2.rest_1_, f32[4,512,128]{2,1,0:T(8,128)S(1)} %far_2.2.rest_2_), custom_call_target="tpu_custom_call" | custom-call | flops 1 | bytes 1 | tf_op jit(solution)/shard_map/far_2/pallas_call | solution.py:189
  66.1 0.0 collective-permute-done.3.refs_1_
  66.1 8.2 %collective-permute-done.4.refs_2_ = bf16[128,1024]{1,0:T(8,128)(2,1)S(1)} collective-permute-done((bf16[128,1024]{1,0:T(8,128)(2,1)S(1)}, bf16[128,1024]{1,0:T(8,128)(2,1)S(1)}, u32[]{:S(2)}, u32[]{:S(2)}) %collective-permute-start.4) | collective-permute-done | bytes 262176 | tf_op jit(solution)/shard_map/ppermute | solution.py:310
  74.3 0.0 collective-permute-done.5.refs_3_
  74.3 0.0 copy-start.7
  74.3 0.7 copy-done.7
  75.0 4.9 %all-to-all-start.1 = ((bf16[4,512,128]{2,1,0:T(8,128)(2,1)}), bf16[4,512,128]{2,1,0:T(8,128)(2,1)S(1)}, u32[]{:S(2)}, u32[]{:S(2)}) async-start(bf16[4,512,128]{2,1,0:T(8,128)(2,1)} %far_2.3), calls=%async_computation.1 | async-start | bytes 1048576 | tf_op jit(solution)/shard_map/all_to_all | solution.py:328
  79.9 0.0 copy-start.8
  79.9 0.9 copy-done.8
  80.9 1.0 join_x.1.refs_0_
  81.9 4.7 %collective-permute-start.6 = (bf16[4,128,1024]{2,1,0:T(8,128)(2,1)S(1)}, bf16[4,128,1024]{2,1,0:T(8,128)(2,1)}, u32[]{:S(2)}, u32[]{:S(2)}) collective-permute-start(bf16[4,128,1024]{2,1,0:T(8,128)(2,1)S(1)} %join_x.1.refs_0_), channel_id=1, source_target_pairs={{0,16},{16,0},{1,17},{17,1},{2,18},{18,2},{3,19},{19,3},{4,20},{20... | collective-permute-start | bytes 3145736 | tf_op jit(solution)/shard_map/ppermute | solution.py:330
  86.6 3.2 %near_2.1.near_ref = f32[512,128]{1,0:T(8,128)S(1)} custom-call(s32[2]{0:T(128)S(1)} %pad_add_fusion.place_ref, bf16[16,2,128,128]{3,2,1,0:T(8,128)(2,1)S(1)} %all-to-all-done.kv_ref, bf16[2112,128]{1,0:T(8,128)(2,1)} %collective-permute-done.1.rest_0_, bf16[2112,128]{1,0:T(8,128)(2,1)} %collective-permute-done.2.rest_1_, f32[512,128]{1,0:T(8,128)S(1)} %near_0.1.rest_2_), custom_call_target="tpu_custom_call" | custom-call | flops 1 | bytes 1 | tf_op jit(solution)/shard_map/near_2/pallas_call | solution.py:218
  89.8 0.0 all-to-all-done.1.part_ref
  89.8 1.0 key_grad.1
  90.8 11.0 %all-to-all-start.2 = ((bf16[8,64,512]{2,1,0:T(8,128)(2,1)}), bf16[8,64,512]{2,1,0:T(8,128)(2,1)S(1)}, u32[]{:S(2)}, u32[]{:S(2)}) async-start(bf16[8,64,512]{2,1,0:T(8,128)(2,1)} %bitcast.19), calls=%async_computation.2 | async-start | bytes 1048576 | tf_op jit(solution)/shard_map/all_to_all | solution.py:333
  101.8 0.0 collective-permute-done.6.refs_1_
  101.8 9.1 %all-to-all-done.2 = bf16[8,64,512]{2,1,0:T(8,128)(2,1)S(1)} async-done(((bf16[8,64,512]{2,1,0:T(8,128)(2,1)}), bf16[8,64,512]{2,1,0:T(8,128)(2,1)S(1)}, u32[]{:S(2)}, u32[]{:S(2)}) %all-to-all-start.2) | async-done | bytes 524320 | tf_op jit(solution)/shard_map/all_to_all | solution.py:333
  110.9 1.9 %project.1 = bf16[16,4,16,256]{3,2,1,0:T(8,128)(2,1)S(1)} custom-call(s32[1]{0:T(128)} %bitcast.core_ref, bf16[2,4,64,512]{3,2,1,0:T(8,128)(2,1)S(1)} %bitcast.35, bf16[4,128,1024]{2,1,0:T(8,128)(2,1)S(1)} %join_x.1.refs_0_, bf16[4,128,1024]{2,1,0:T(8,128)(2,1)} %collective-permute-done.6.refs_1_), custom_call_target="tpu_custom_call" | custom-call | tf_op jit(solution)/shard_map/project/pallas_call | solution.py:267
  112.8 31.5 %all_to_all.20.part_ref = bf16[64,16,256]{2,1,0:T(8,128)(2,1)S(1)} all-to-all(bf16[64,16,256]{2,1,0:T(8,128)(2,1)S(1)} %bitcast.36), channel_id=1, replica_groups=mesh['yh'=4,'x'=4,'core'=2,'zh'=4,'zl'=2,'yl'=2] {'yh','x','zh'}, dimensions={0} | all-to-all | bytes 1048576 | tf_op jit(solution)/shard_map/all_to_all | solution.py:335
  144.3 0.7 total.1
Async XLA Ops:
  0.7 14.3 %copy-start.6 = (f32[1,128,32]{1,2,0:T(8,128)S(1)}, f32[1,128,32]{1,2,0:T(8,128)}, u32[]{:S(2)}) copy-start(f32[1,128,32]{1,2,0:T(8,128)} %param.14) | copy-start | bytes 49156
  2.8 12.2 %copy-start = (bf16[1,128,4096]{2,1,0:T(8,128)(2,1)S(1)}, bf16[1,128,4096]{2,1,0:T(8,128)(2,1)}, u32[]{:S(2)}) copy-start(bf16[1,128,4096]{2,1,0:T(8,128)(2,1)} %param.9) | copy-start | bytes 3145732
  2.8 12.2 %copy-start.1 = (bf16[1,128,4096]{2,1,0:T(8,128)(2,1)S(1)}, bf16[1,128,4096]{2,1,0:T(8,128)(2,1)}, u32[]{:S(2)}) copy-start(bf16[1,128,4096]{2,1,0:T(8,128)(2,1)} %param.10) | copy-start | bytes 3145732
  2.8 40.6 %all-to-all-start = ((bf16[16,2,128,128]{3,2,1,0:T(8,128)(2,1)}), bf16[16,2,128,128]{3,2,1,0:T(8,128)(2,1)S(1)}, u32[]{:S(2)}, u32[]{:S(2)}) async-start(bf16[16,2,128,128]{3,2,1,0:T(8,128)(2,1)} %bitcast.46), calls=%async_computation | async-start | bytes 2097152 | tf_op jit(solution)/shard_map/all_to_all | solution.py:304
  14.9 0.7 copy-start.5
  16.6 26.8 %collective-permute-start = (bf16[2112,128]{1,0:T(8,128)(2,1)}, bf16[2112,128]{1,0:T(8,128)(2,1)}, u32[]{:S(2)}, u32[]{:S(2)}) collective-permute-start(bf16[2112,128]{1,0:T(8,128)(2,1)} %pack_q.4), channel_id=1, source_target_pairs={{0,1},{1,0},{2,3},{3,2},{4,5},{5,4},{6,7},{7,6},{8,9},{9,8},{10,11... | collective-permute-start | bytes 1622024 | tf_op jit(solution)/shard_map/ppermute | solution.py:310
  20.8 43.2 %collective-permute-start.1 = (bf16[2112,128]{1,0:T(8,128)(2,1)}, bf16[2112,128]{1,0:T(8,128)(2,1)}, u32[]{:S(2)}, u32[]{:S(2)}) collective-permute-start(bf16[2112,128]{1,0:T(8,128)(2,1)} %pack_q.6), channel_id=1, source_target_pairs={{0,2},{1,3},{2,0},{3,1},{4,6},{5,7},{6,4},{7,5},{8,10},{9,11},{10,... | collective-permute-start | bytes 1622024 | tf_op jit(solution)/shard_map/ppermute | solution.py:310
  23.9 2.9 %copy-start.4 = (bf16[1,128,4096]{2,1,0:T(8,128)(2,1)S(1)}, bf16[1,128,4096]{2,1,0:T(8,128)(2,1)}, u32[]{:S(2)}) copy-start(bf16[1,128,4096]{2,1,0:T(8,128)(2,1)} %param.15) | copy-start | bytes 3145732
  24.8 39.2 %collective-permute-start.2 = (bf16[2112,128]{1,0:T(8,128)(2,1)}, bf16[2112,128]{1,0:T(8,128)(2,1)}, u32[]{:S(2)}, u32[]{:S(2)}) collective-permute-start(bf16[2112,128]{1,0:T(8,128)(2,1)} %pack_q.7), channel_id=1, source_target_pairs={{0,3},{1,2},{2,1},{3,0},{4,7},{5,6},{6,5},{7,4},{8,11},{9,10},{10,... | collective-permute-start | bytes 1622024 | tf_op jit(solution)/shard_map/ppermute | solution.py:310
  27.7 0.7 copy-start.9
  28.4 0.7 copy-start.11
  29.1 37.0 %collective-permute-start.3 = (bf16[128,1024]{1,0:T(8,128)(2,1)}, bf16[128,1024]{1,0:T(8,128)(2,1)}, u32[]{:S(2)}, u32[]{:S(2)}) collective-permute-start(bf16[128,1024]{1,0:T(8,128)(2,1)} %get-tuple-element.34), channel_id=1, source_target_pairs={{0,1},{1,0},{2,3},{3,2},{4,5},{5,4},{6,7},{7,6},{8,9},{9,8},{10,11... | collective-permute-start | bytes 786440 | tf_op jit(solution)/shard_map/ppermute | solution.py:310
  32.6 0.8 copy-start.2
  43.4 1.0 copy-start.3
  47.5 1.2 copy-start.12
  47.5 5.1 %copy-start.10 = (bf16[128,1024]{1,0:T(8,128)(2,1)S(1)}, bf16[128,1024]{1,0:T(8,128)(2,1)}, u32[]{:S(2)}) copy-start(bf16[128,1024]{1,0:T(8,128)(2,1)} %copy-done.9) | copy-start | bytes 786436
  48.7 25.6 %collective-permute-start.4 = (bf16[128,1024]{1,0:T(8,128)(2,1)S(1)}, bf16[128,1024]{1,0:T(8,128)(2,1)S(1)}, u32[]{:S(2)}, u32[]{:S(2)}) collective-permute-start(bf16[128,1024]{1,0:T(8,128)(2,1)S(1)} %copy-done.12), channel_id=1, source_target_pairs={{0,2},{1,3},{2,0},{3,1},{4,6},{5,7},{6,4},{7,5},{8,10},{9,11},{10,... | collective-permute-start | bytes 786440 | tf_op jit(solution)/shard_map/ppermute | solution.py:310
  52.6 21.7 %collective-permute-start.5 = (bf16[128,1024]{1,0:T(8,128)(2,1)S(1)}, bf16[128,1024]{1,0:T(8,128)(2,1)S(1)}, u32[]{:S(2)}, u32[]{:S(2)}) collective-permute-start(bf16[128,1024]{1,0:T(8,128)(2,1)S(1)} %copy-done.10), channel_id=1, source_target_pairs={{0,3},{1,2},{2,1},{3,0},{4,7},{5,6},{6,5},{7,4},{8,11},{9,10},{10,... | collective-permute-start | bytes 786440 | tf_op jit(solution)/shard_map/ppermute | solution.py:310
  74.3 0.7 copy-start.7
  75.0 14.8 %all-to-all-start.1 = ((bf16[4,512,128]{2,1,0:T(8,128)(2,1)}), bf16[4,512,128]{2,1,0:T(8,128)(2,1)S(1)}, u32[]{:S(2)}, u32[]{:S(2)}) async-start(bf16[4,512,128]{2,1,0:T(8,128)(2,1)} %far_2.3), calls=%async_computation.1 | async-start | bytes 1048576 | tf_op jit(solution)/shard_map/all_to_all | solution.py:328
  79.9 0.9 copy-start.8
  81.9 19.9 %collective-permute-start.6 = (bf16[4,128,1024]{2,1,0:T(8,128)(2,1)S(1)}, bf16[4,128,1024]{2,1,0:T(8,128)(2,1)}, u32[]{:S(2)}, u32[]{:S(2)}) collective-permute-start(bf16[4,128,1024]{2,1,0:T(8,128)(2,1)S(1)} %join_x.1.refs_0_), channel_id=1, source_target_pairs={{0,16},{16,0},{1,17},{17,1},{2,18},{18,2},{3,19},{19,3},{4,20},{20... | collective-permute-start | bytes 3145736 | tf_op jit(solution)/shard_map/ppermute | solution.py:330
  90.8 20.1 %all-to-all-start.2 = ((bf16[8,64,512]{2,1,0:T(8,128)(2,1)}), bf16[8,64,512]{2,1,0:T(8,128)(2,1)S(1)}, u32[]{:S(2)}, u32[]{:S(2)}) async-start(bf16[8,64,512]{2,1,0:T(8,128)(2,1)} %bitcast.19), calls=%async_computation.2 | async-start | bytes 1048576 | tf_op jit(solution)/shard_map/all_to_all | solution.py:333
